TPU v7x, 512 devices: a whole 4x8x8 slice. The times are simulated.
512 devices in a mesh: band: 8 (over y_lo, core), lon: 64 (over y_hi, x, z).
Axes of the slice: x: 4, y: 8 (y_hi: 2, y_lo: 4; y = y_hi * 4 + y_lo), z: 8, core: 2. Of those that a mesh axis runs over, the one named last changes fastest.
Arguments:
- e_field: float32 [3, 8, 64, 8192], P(None, None, 'band', 'lon'), may hold values from -10 to 10
- h_field: float32 [3, 8, 64, 8192], P(None, None, 'band', 'lon'), may hold values from -10 to 10
- conductivity: float32 [9, 8, 64, 8192], P(None, None, 'band', 'lon'), as said below
- zone_factor: int32 [8], replicated, may hold values from 1 to 8, as said below
- zone_bounds: int32 [7], replicated, may hold values from 1 to 63, as said below
Outputs:
- e_final: float32 [3, 8, 64, 8192], P(None, None, 'band', 'lon')
- h_final: float32 [3, 8, 64, 8192], P(None, None, 'band', 'lon')
Inputs may be any that keep to these rules, and one draw needn't show every extreme that they name: `zone_factor`: every entry is a power of two. `zone_bounds`: strictly increasing; the first entry is 1 and the last is 63. `conductivity`: per cell the symmetric part of the 3 x 3 tensor is positive semidefinite.
All inputs are finite; a program needn't handle non-finite values.
Results may differ from a plain program's by a relative error of at most 0.0001.
Values sent between devices are 32-bit elements; how exact they have to be, the bound alone decides.
A program may use at most 64 MiB of HBM per device.

v0:
```python
import jax
import jax.numpy as jnp
from jax import lax
from jax.sharding import PartitionSpec as P

STEPS = 4


north_coef = 0.45
radial_coef = 0.5
east_coef = 0.12
metric_floor = 0.25


def from_behind(value, axis, by):
    length = lax.axis_size(axis)
    pairs = [(i, i + by) for i in range(length) if 0 <= i + by < length]
    return lax.ppermute(value, axis, pairs)


def shifted(value, axis, steps):
    count = lax.axis_size(axis)
    pairs = [(source, (source + steps) % count) for source in range(count)]
    return lax.ppermute(value, axis, pairs)


def inverse_parts(conduct):
    matrix = [
        [conduct[0] + 1.0, conduct[1], conduct[2]],
        [conduct[3], conduct[4] + 1.0, conduct[5]],
        [conduct[6], conduct[7], conduct[8] + 1.0],
    ]

    def cofactor(across, within):
        upper_row = (across + 1) % 3
        lower_row = (across + 2) % 3
        left_col = (within + 1) % 3
        right_col = (within + 2) % 3
        return (
            matrix[upper_row][left_col] * matrix[lower_row][right_col]
            - matrix[upper_row][right_col] * matrix[lower_row][left_col]
        )

    determ = (
        matrix[0][0] * cofactor(0, 0)
        + matrix[0][1] * cofactor(0, 1)
        + matrix[0][2] * cofactor(0, 2)
    )
    inverse_det = 1.0 / determ
    return jnp.stack(
        [cofactor(within, across) * inverse_det for across in range(3) for within in range(3)]
    )


def apply_update(update, drive_term):
    return jnp.stack(
        [
            update[3 * across] * drive_term[0]
            + update[3 * across + 1] * drive_term[1]
            + update[3 * across + 2] * drive_term[2]
            for across in range(3)
        ]
    )


def row_factors(zone_factor, zone_bounds, first_row, row_count, total_rows):
    rows_here = first_row + jnp.arange(row_count, dtype=jnp.int32)
    zone_of = jnp.sum((rows_here[:, None] >= zone_bounds[None, :]).astype(jnp.int32), axis=1)
    picked = zone_of[:, None] == jnp.arange(zone_factor.shape[0], dtype=jnp.int32)[None, :]
    factor = jnp.sum(jnp.where(picked, zone_factor[None, :], 0), axis=1)
    latitude = ((rows_here.astype(jnp.float32) + 0.5) / total_rows - 0.5) * jnp.pi
    metric = east_coef / jnp.maximum(factor.astype(jnp.float32) * jnp.cos(latitude), metric_floor)
    return (factor, metric)


def curl_parts(north_diff, east_diff, radial_diff):
    return jnp.stack(
        [
            north_diff[2] - radial_diff[1],
            radial_diff[0] - east_diff[2],
            east_diff[1] - north_diff[0],
        ]
    )


def forward_curl(grid_field, lat_rim, lon_rim, metric_grid):
    north_next = jnp.concatenate([grid_field[:, :, 1:, :], lat_rim[:, :, None, :]], axis=2)
    east_next = jnp.concatenate([grid_field[:, :, :, 1:], lon_rim[:, :, :, None]], axis=3)
    upper_layer = jnp.concatenate([grid_field[:, 1:], jnp.zeros_like(grid_field[:, :1])], axis=1)
    return curl_parts(
        north_coef * (north_next - grid_field),
        metric_grid * (east_next - grid_field),
        radial_coef * (upper_layer - grid_field),
    )


def backward_curl(grid_field, lat_rim, lon_rim, metric_grid):
    south_prev = jnp.concatenate([lat_rim[:, :, None, :], grid_field[:, :, :-1, :]], axis=2)
    west_prev = jnp.concatenate([lon_rim[:, :, :, None], grid_field[:, :, :, :-1]], axis=3)
    lower_layer = jnp.concatenate([jnp.zeros_like(grid_field[:, :1]), grid_field[:, :-1]], axis=1)
    return curl_parts(
        north_coef * (grid_field - south_prev),
        metric_grid * (grid_field - west_prev),
        radial_coef * (grid_field - lower_layer),
    )


def merge_rows(grid_field, factor):
    lon_cells = grid_field.shape[-1]
    result = grid_field
    for group_size in (2, 4, 8):
        grouped = grid_field.reshape(grid_field.shape[:-1] + (lon_cells // group_size, group_size))
        averages = jnp.sum(grouped, axis=-1) / group_size
        spread_out = jnp.repeat(averages, group_size, axis=-1)
        result = jnp.where((factor == group_size)[None, None, :, None], spread_out, result)
    return result


def cap_mean(pole_row, lon_total):
    totals = lax.psum(jnp.sum(pole_row, axis=-1), "lon")
    return totals / lon_total


def on_device(e_field, h_field, conductivity, zone_factor, zone_bounds):
    band_count = lax.axis_size("band")
    band_place = lax.axis_index("band")
    rows_dev = e_field.shape[2]
    lon_cells = e_field.shape[3]
    lon_total = lon_cells * lax.axis_size("lon")
    at_north = band_place == band_count - 1
    at_south = band_place == 0
    factor, metric = row_factors(
        zone_factor, zone_bounds, band_place * rows_dev, rows_dev, rows_dev * band_count
    )
    metric_grid = metric[None, None, :, None]
    update = inverse_parts(conductivity)
    electric = e_field
    magnetic = h_field
    for step_idx in range(STEPS):
        above_rows = from_behind(electric[:, :, 0, :], "band", -1)
        cap_north = cap_mean(electric[:, :, -1, :], lon_total)
        north_rim = jnp.where(
            at_north, jnp.broadcast_to(cap_north[:, :, None], above_rows.shape), above_rows
        )
        east_rim = shifted(electric[:, :, :, 0], "lon", -1)
        magnetic = merge_rows(
            magnetic - forward_curl(electric, north_rim, east_rim, metric_grid), factor
        )
        below_rows = from_behind(magnetic[:, :, -1, :], "band", 1)
        cap_south = cap_mean(magnetic[:, :, 0, :], lon_total)
        south_rim = jnp.where(
            at_south, jnp.broadcast_to(cap_south[:, :, None], below_rows.shape), below_rows
        )
        west_rim = shifted(magnetic[:, :, :, -1], "lon", 1)
        drive_term = 2.0 * electric + backward_curl(magnetic, south_rim, west_rim, metric_grid)
        electric = merge_rows(apply_update(update, drive_term) - electric, factor)
    return (electric, magnetic)


def solution(mesh):
    placed = (
        P(None, None, "band", "lon"),
        P(None, None, "band", "lon"),
        P(None, None, "band", "lon"),
        P(),
        P(),
    )
    return jax.shard_map(
        on_device,
        mesh=mesh,
        in_specs=placed,
        out_specs=(P(None, None, "band", "lon"), P(None, None, "band", "lon")),
        check_vma=False,
    )
```

profile of v0, /device:TPU:1, one launch (start us, length us, event | category | flops | bytes accessed | tf_op | source)
XLA Modules:
  0.0 1939.4 jit_solution(311208050225594095)
XLA Ops:
  1.8 19.0 collective-permute-start.1
  21.7 2.9 collective-permute-start
  27.3 187.8 %psum.56 = f32[3,8]{1,0:T(4,128)S(1)} all-reduce(f32[3,8]{1,0:T(4,128)S(1)} %slice_reduce_fusion.13), channel_id=1, replica_groups=mesh['band'=8,'lon'=64] {'lon'}, use_global_device_ids=true, to_apply=%region_3.4 | all-reduce | flops 24 | bytes 192 | tf_op jit(solution)/shard_map/psum | solution.py:120
  222.2 188.4 %psum.57 = f32[3,8]{1,0:T(4,128)S(1)} all-reduce(f32[3,8]{1,0:T(4,128)S(1)} %slice_reduce_fusion.12), channel_id=1, replica_groups=mesh['band'=8,'lon'=64] {'lon'}, use_global_device_ids=true, to_apply=%region_8.9 | all-reduce | flops 24 | bytes 192 | tf_op jit(solution)/shard_map/psum | solution.py:120
  410.6 2.6 collective-permute-start.3
  413.2 58.1 %collective-permute-start.2 = (f32[3,8,128]{2,1,0:T(8,128)S(1)}, f32[3,8,128]{2,1,0:T(8,128)S(1)}, u32[]{:S(2)}, u32[]{:S(2)}) collective-permute-start(f32[3,8,128]{2,1,0:T(8,128)S(1)} %slice_bitcast_fusion.5), channel_id=1, source_target_pairs={{0,64},{64,128},{128,192},{192,256},{256,320},{320,384},{384,448},... | collective-permute-start | bytes 36872 | tf_op jit(solution)/shard_map/ppermute | solution.py:18
  478.7 196.6 %psum.58 = f32[3,8]{1,0:T(4,128)S(1)} all-reduce(f32[3,8]{1,0:T(4,128)S(1)} %get-tuple-element.86), channel_id=1, replica_groups=mesh['band'=8,'lon'=64] {'lon'}, use_global_device_ids=true, to_apply=%region_13.14 | all-reduce | flops 24 | bytes 192 | tf_op jit(solution)/shard_map/psum | solution.py:120
  675.3 27.7 %collective-permute-start.4 = (f32[3,8,128]{2,1,0:T(8,128)S(1)}, f32[3,8,128]{2,1,0:T(8,128)S(1)}, u32[]{:S(2)}, u32[]{:S(2)}) collective-permute-start(f32[3,8,128]{2,1,0:T(8,128)S(1)} %get-tuple-element.87), channel_id=1, source_target_pairs={{64,0},{128,64},{192,128},{256,192},{320,256},{384,320},{448,384},... | collective-permute-start | bytes 36872 | tf_op jit(solution)/shard_map/ppermute | solution.py:18
  703.0 3.8 collective-permute-start.5
  720.3 196.0 %psum.59 = f32[3,8]{1,0:T(4,128)S(1)} all-reduce(f32[3,8]{1,0:T(4,128)S(1)} %slice_reduce_fusion.10), channel_id=1, replica_groups=mesh['band'=8,'lon'=64] {'lon'}, use_global_device_ids=true, to_apply=%region_18.19 | all-reduce | flops 24 | bytes 192 | tf_op jit(solution)/shard_map/psum | solution.py:120
  916.2 1.9 collective-permute-start.7
  918.2 33.4 %collective-permute-start.6 = (f32[3,8,128]{2,1,0:T(8,128)S(1)}, f32[3,8,128]{2,1,0:T(8,128)S(1)}, u32[]{:S(2)}, u32[]{:S(2)}) collective-permute-start(f32[3,8,128]{2,1,0:T(8,128)S(1)} %slice_bitcast_fusion.3), channel_id=1, source_target_pairs={{0,64},{64,128},{128,192},{192,256},{256,320},{320,384},{384,448},... | collective-permute-start | bytes 36872 | tf_op jit(solution)/shard_map/ppermute | solution.py:18
  958.8 197.1 %psum.60 = f32[3,8]{1,0:T(4,128)S(1)} all-reduce(f32[3,8]{1,0:T(4,128)S(1)} %slice_reduce_fusion.9), channel_id=1, replica_groups=mesh['band'=8,'lon'=64] {'lon'}, use_global_device_ids=true, to_apply=%region_23.24 | all-reduce | flops 24 | bytes 192 | tf_op jit(solution)/shard_map/psum | solution.py:120
  1157.8 27.9 %collective-permute-start.8 = (f32[3,8,128]{2,1,0:T(8,128)S(1)}, f32[3,8,128]{2,1,0:T(8,128)S(1)}, u32[]{:S(2)}, u32[]{:S(2)}) collective-permute-start(f32[3,8,128]{2,1,0:T(8,128)S(1)} %slice_bitcast_fusion.2), channel_id=1, source_target_pairs={{64,0},{128,64},{192,128},{256,192},{320,256},{384,320},{448,384},... | collective-permute-start | bytes 36872 | tf_op jit(solution)/shard_map/ppermute | solution.py:18
  1186.1 5.2 collective-permute-done.8
  1203.5 189.0 %psum.61 = f32[3,8]{1,0:T(4,128)S(1)} all-reduce(f32[3,8]{1,0:T(4,128)S(1)} %slice_reduce_fusion.8), channel_id=1, replica_groups=mesh['band'=8,'lon'=64] {'lon'}, use_global_device_ids=true, to_apply=%region_28.29 | all-reduce | flops 24 | bytes 192 | tf_op jit(solution)/shard_map/psum | solution.py:120
  1394.5 36.5 %collective-permute-start.10 = (f32[3,8,128]{2,1,0:T(8,128)S(1)}, f32[3,8,128]{2,1,0:T(8,128)S(1)}, u32[]{:S(2)}, u32[]{:S(2)}) collective-permute-start(f32[3,8,128]{2,1,0:T(8,128)S(1)} %slice_bitcast_fusion.1), channel_id=1, source_target_pairs={{0,64},{64,128},{128,192},{192,256},{256,320},{320,384},{384,448},... | collective-permute-start | bytes 36872 | tf_op jit(solution)/shard_map/ppermute | solution.py:18
  1444.2 197.2 %psum.62 = f32[3,8]{1,0:T(4,128)S(1)} all-reduce(f32[3,8]{1,0:T(4,128)S(1)} %slice_reduce_fusion.7), channel_id=1, replica_groups=mesh['band'=8,'lon'=64] {'lon'}, use_global_device_ids=true, to_apply=%region_33.34 | all-reduce | flops 24 | bytes 192 | tf_op jit(solution)/shard_map/psum | solution.py:120
  1643.2 26.7 %collective-permute-start.12 = (f32[3,8,128]{2,1,0:T(8,128)S(1)}, f32[3,8,128]{2,1,0:T(8,128)S(1)}, u32[]{:S(2)}, u32[]{:S(2)}) collective-permute-start(f32[3,8,128]{2,1,0:T(8,128)S(1)} %slice_bitcast_fusion), channel_id=1, source_target_pairs={{64,0},{128,64},{192,128},{256,192},{320,256},{384,320},{448,384},... | collective-permute-start | bytes 36872 | tf_op jit(solution)/shard_map/ppermute | solution.py:18
  1670.3 6.3 collective-permute-done.12
  1688.9 188.9 %psum.63 = f32[3,8]{1,0:T(4,128)S(1)} all-reduce(f32[3,8]{1,0:T(4,128)S(1)} %get-tuple-element.44), channel_id=1, replica_groups=mesh['band'=8,'lon'=64] {'lon'}, use_global_device_ids=true, to_apply=%region_38.39 | all-reduce | flops 24 | bytes 192 | tf_op jit(solution)/shard_map/psum | solution.py:120
  1877.8 36.6 %collective-permute-start.14 = (f32[3,8,128]{2,1,0:T(8,128)S(1)}, f32[3,8,128]{2,1,0:T(8,128)S(1)}, u32[]{:S(2)}, u32[]{:S(2)}) collective-permute-start(f32[3,8,128]{2,1,0:T(8,128)S(1)} %bitcast.163), channel_id=1, source_target_pairs={{0,64},{64,128},{128,192},{192,256},{256,320},{320,384},{384,448},... | collective-permute-start | bytes 36872 | tf_op jit(solution)/shard_map/ppermute | solution.py:18
  1914.4 1.9 collective-permute-start.15
  1916.3 10.6 collective-permute-done.15
  (397 shorter events, 94.2 us)
Async XLA Ops:
  1.8 214.4 %collective-permute-start.1 = (f32[3,8,8]{2,1,0:T(8,128)S(1)}, f32[3,8,8]{2,1,0:T(8,128)S(1)}, u32[]{:S(2)}, u32[]{:S(2)}) collective-permute-start(f32[3,8,8]{2,1,0:T(8,128)S(1)} %bitcast.162), channel_id=1, source_target_pairs={{0,63},{1,0},{2,1},{3,2},{4,3},{5,4},{6,5},{7,6},{8,7},{9,8},{10,9... | collective-permute-start | bytes 2312 | tf_op jit(solution)/shard_map/ppermute | solution.py:24
  21.7 194.7 %collective-permute-start = (f32[3,8,128]{2,1,0:T(8,128)S(1)}, f32[3,8,128]{2,1,0:T(8,128)S(1)}, u32[]{:S(2)}, u32[]{:S(2)}) collective-permute-start(f32[3,8,128]{2,1,0:T(8,128)S(1)} %slice_bitcast_fusion.6), channel_id=1, source_target_pairs={{64,0},{128,64},{192,128},{256,192},{320,256},{384,320},{448,384},... | collective-permute-start | bytes 36872 | tf_op jit(solution)/shard_map/ppermute | solution.py:18
  410.6 60.8 %collective-permute-start.3 = (f32[3,8,8]{2,1,0:T(8,128)S(1)}, f32[3,8,8]{2,1,0:T(8,128)S(1)}, u32[]{:S(2)}, u32[]{:S(2)}) collective-permute-start(f32[3,8,8]{2,1,0:T(8,128)S(1)} %slice_reduce_fusion.5), channel_id=1, source_target_pairs={{0,1},{1,2},{2,3},{3,4},{4,5},{5,6},{6,7},{7,8},{8,9},{9,10},{10,1... | collective-permute-start | bytes 2312 | tf_op jit(solution)/shard_map/ppermute | solution.py:24
  413.2 59.0 %collective-permute-start.2 = (f32[3,8,128]{2,1,0:T(8,128)S(1)}, f32[3,8,128]{2,1,0:T(8,128)S(1)}, u32[]{:S(2)}, u32[]{:S(2)}) collective-permute-start(f32[3,8,128]{2,1,0:T(8,128)S(1)} %slice_bitcast_fusion.5), channel_id=1, source_target_pairs={{0,64},{64,128},{128,192},{192,256},{256,320},{320,384},{384,448},... | collective-permute-start | bytes 36872 | tf_op jit(solution)/shard_map/ppermute | solution.py:18
  472.5 480.1 %copy-start.7 = (f32[1,8,8,128]{3,1,0,2:T(8,128)}, f32[1,8,8,128]{3,1,0,2:T(8,128)S(1)}, u32[]{:S(2)}) copy-start(f32[1,8,8,128]{3,1,0,2:T(8,128)S(1)} %get-tuple-element.3) | copy-start | bytes 98308
  472.5 480.1 %copy-start.10 = (f32[1,8,8,128]{3,1,0,2:T(8,128)}, f32[1,8,8,128]{3,1,0,2:T(8,128)S(1)}, u32[]{:S(2)}) copy-start(f32[1,8,8,128]{3,1,0,2:T(8,128)S(1)} %get-tuple-element.4) | copy-start | bytes 98308
  472.5 480.1 %copy-start.13 = (f32[1,8,8,128]{3,1,0,2:T(8,128)}, f32[1,8,8,128]{3,1,0,2:T(8,128)S(1)}, u32[]{:S(2)}) copy-start(f32[1,8,8,128]{3,1,0,2:T(8,128)S(1)} %get-tuple-element.5) | copy-start | bytes 98308
  675.3 33.4 %collective-permute-start.4 = (f32[3,8,128]{2,1,0:T(8,128)S(1)}, f32[3,8,128]{2,1,0:T(8,128)S(1)}, u32[]{:S(2)}, u32[]{:S(2)}) collective-permute-start(f32[3,8,128]{2,1,0:T(8,128)S(1)} %get-tuple-element.87), channel_id=1, source_target_pairs={{64,0},{128,64},{192,128},{256,192},{320,256},{384,320},{448,384},... | collective-permute-start | bytes 36872 | tf_op jit(solution)/shard_map/ppermute | solution.py:18
  703.0 4.6 collective-permute-start.5
  916.2 35.4 %collective-permute-start.7 = (f32[3,8,8]{2,1,0:T(8,128)S(1)}, f32[3,8,8]{2,1,0:T(8,128)S(1)}, u32[]{:S(2)}, u32[]{:S(2)}) collective-permute-start(f32[3,8,8]{2,1,0:T(8,128)S(1)} %slice_reduce_fusion.4), channel_id=1, source_target_pairs={{0,1},{1,2},{2,3},{3,4},{4,5},{5,6},{6,7},{7,8},{8,9},{9,10},{10,1... | collective-permute-start | bytes 2312 | tf_op jit(solution)/shard_map/ppermute | solution.py:24
  918.2 34.2 %collective-permute-start.6 = (f32[3,8,128]{2,1,0:T(8,128)S(1)}, f32[3,8,128]{2,1,0:T(8,128)S(1)}, u32[]{:S(2)}, u32[]{:S(2)}) collective-permute-start(f32[3,8,128]{2,1,0:T(8,128)S(1)} %slice_bitcast_fusion.3), channel_id=1, source_target_pairs={{0,64},{64,128},{128,192},{192,256},{256,320},{320,384},{384,448},... | collective-permute-start | bytes 36872 | tf_op jit(solution)/shard_map/ppermute | solution.py:18
  1155.8 30.0 %collective-permute-start.9 = (f32[3,8,8]{2,1,0:T(8,128)S(1)}, f32[3,8,8]{2,1,0:T(8,128)S(1)}, u32[]{:S(2)}, u32[]{:S(2)}) collective-permute-start(f32[3,8,8]{2,1,0:T(8,128)S(1)} %slice_reduce_fusion.3), channel_id=1, source_target_pairs={{0,63},{1,0},{2,1},{3,2},{4,3},{5,4},{6,5},{7,6},{8,7},{9,8},{10,9... | collective-permute-start | bytes 2312 | tf_op jit(solution)/shard_map/ppermute | solution.py:24
  1157.8 33.5 %collective-permute-start.8 = (f32[3,8,128]{2,1,0:T(8,128)S(1)}, f32[3,8,128]{2,1,0:T(8,128)S(1)}, u32[]{:S(2)}, u32[]{:S(2)}) collective-permute-start(f32[3,8,128]{2,1,0:T(8,128)S(1)} %slice_bitcast_fusion.2), channel_id=1, source_target_pairs={{64,0},{128,64},{192,128},{256,192},{320,256},{384,320},{448,384},... | collective-permute-start | bytes 36872 | tf_op jit(solution)/shard_map/ppermute | solution.py:18
  1392.6 38.5 %collective-permute-start.11 = (f32[3,8,8]{2,1,0:T(8,128)S(1)}, f32[3,8,8]{2,1,0:T(8,128)S(1)}, u32[]{:S(2)}, u32[]{:S(2)}) collective-permute-start(f32[3,8,8]{2,1,0:T(8,128)S(1)} %slice_reduce_fusion.2), channel_id=1, source_target_pairs={{0,1},{1,2},{2,3},{3,4},{4,5},{5,6},{6,7},{7,8},{8,9},{9,10},{10,1... | collective-permute-start | bytes 2312 | tf_op jit(solution)/shard_map/ppermute | solution.py:24
  1394.5 37.3 %collective-permute-start.10 = (f32[3,8,128]{2,1,0:T(8,128)S(1)}, f32[3,8,128]{2,1,0:T(8,128)S(1)}, u32[]{:S(2)}, u32[]{:S(2)}) collective-permute-start(f32[3,8,128]{2,1,0:T(8,128)S(1)} %slice_bitcast_fusion.1), channel_id=1, source_target_pairs={{0,64},{64,128},{128,192},{192,256},{256,320},{320,384},{384,448},... | collective-permute-start | bytes 36872 | tf_op jit(solution)/shard_map/ppermute | solution.py:18
  1641.3 28.8 %collective-permute-start.13 = (f32[3,8,8]{2,1,0:T(8,128)S(1)}, f32[3,8,8]{2,1,0:T(8,128)S(1)}, u32[]{:S(2)}, u32[]{:S(2)}) collective-permute-start(f32[3,8,8]{2,1,0:T(8,128)S(1)} %slice_reduce_fusion.1), channel_id=1, source_target_pairs={{0,63},{1,0},{2,1},{3,2},{4,3},{5,4},{6,5},{7,6},{8,7},{9,8},{10,9... | collective-permute-start | bytes 2312 | tf_op jit(solution)/shard_map/ppermute | solution.py:24
  1643.2 33.4 %collective-permute-start.12 = (f32[3,8,128]{2,1,0:T(8,128)S(1)}, f32[3,8,128]{2,1,0:T(8,128)S(1)}, u32[]{:S(2)}, u32[]{:S(2)}) collective-permute-start(f32[3,8,128]{2,1,0:T(8,128)S(1)} %slice_bitcast_fusion), channel_id=1, source_target_pairs={{64,0},{128,64},{192,128},{256,192},{320,256},{384,320},{448,384},... | collective-permute-start | bytes 36872 | tf_op jit(solution)/shard_map/ppermute | solution.py:18
  1687.6 239.8 %copy-start.28 = (f32[3,8,8,128]{3,1,0,2:T(8,128)S(1)}, f32[3,8,8,128]{3,1,0,2:T(8,128)}, u32[]{:S(2)}) copy-start(f32[3,8,8,128]{3,1,0,2:T(8,128)} %get-tuple-element.36) | copy-start | bytes 294916
  1688.4 239.1 %copy-start.9 = (f32[1,8,8,128]{3,1,0,2:T(8,128)S(1)}, f32[1,8,8,128]{3,1,0,2:T(8,128)}, u32[]{:S(2)}) copy-start(f32[1,8,8,128]{3,1,0,2:T(8,128)} %copy-done.7) | copy-start | bytes 98308
  1688.4 239.1 %copy-start.12 = (f32[1,8,8,128]{3,1,0,2:T(8,128)S(1)}, f32[1,8,8,128]{3,1,0,2:T(8,128)}, u32[]{:S(2)}) copy-start(f32[1,8,8,128]{3,1,0,2:T(8,128)} %copy-done.10) | copy-start | bytes 98308
  1688.4 239.1 %copy-start.15 = (f32[1,8,8,128]{3,1,0,2:T(8,128)S(1)}, f32[1,8,8,128]{3,1,0,2:T(8,128)}, u32[]{:S(2)}) copy-start(f32[1,8,8,128]{3,1,0,2:T(8,128)} %copy-done.13) | copy-start | bytes 98308
  1688.5 240.2 %copy-start.1 = (f32[3,8,8,128]{3,2,1,0:T(8,128)}, f32[3,8,8,128]{3,2,1,0:T(8,128)S(1)}, u32[]{:S(2)}) copy-start(f32[3,8,8,128]{3,2,1,0:T(8,128)S(1)} %select_select_fusion.1) | copy-start | bytes 294916
  1877.8 49.4 %collective-permute-start.14 = (f32[3,8,128]{2,1,0:T(8,128)S(1)}, f32[3,8,128]{2,1,0:T(8,128)S(1)}, u32[]{:S(2)}, u32[]{:S(2)}) collective-permute-start(f32[3,8,128]{2,1,0:T(8,128)S(1)} %bitcast.163), channel_id=1, source_target_pairs={{0,64},{64,128},{128,192},{192,256},{256,320},{320,384},{384,448},... | collective-permute-start | bytes 36872 | tf_op jit(solution)/shard_map/ppermute | solution.py:18
  1914.4 12.6 collective-permute-start.15
  (58 other events, 3496.8 us)
where the time goes:
time: 1950 us; the launch traced here: 1940 us
  blocking collectives  1540 us (79%)
  starting transfers between devices  285 us (15%)
  local copies, waits for them, and re-layouts  49.3 us (3%)
  other arithmetic  36.1 us (2%)
  waiting for transfers between devices  25.2 us (1%)
    psum x8, blocking collectives, cap_mean(): totals = lax.psum(jnp.sum(pole_row, axis=-1), 'lon')  1540 us
    ppermute x8, starting transfers between devices, from_behind(): return lax.ppermute(value, axis, pairs)  250 us
  transfers between devices with their start and end apart: 16, of which 8 were waited for; matrix products, arithmetic and copies ran while one was open for 0% of the time, Pallas kernels for 0%

commit v1 on v0

v1 whole, which is shorter than its diff:
```python
import functools

import jax
import jax.numpy as jnp
from jax import lax
from jax.experimental import pallas as pl
from jax.experimental.pallas import tpu as pltpu
from jax.sharding import PartitionSpec as P

MESH = pl.DeviceIdType.MESH
STEPS = 4
NORTH, RADIAL, EAST, FLOOR = 0.45, 0.5, 0.12, 0.25
FIELDS = 15


def lane_ids():
    return lax.broadcasted_iota(jnp.int32, (8, 128), 1)


def row_ids():
    return lax.broadcasted_iota(jnp.int32, (8, 128), 0)


def roll(x, by, axis):
    by = by % x.shape[axis]
    return x if by == 0 else pltpu.roll(x, by, axis)


def pair_shift(main, edge, by, axis):
    ids = lane_ids() if axis == 1 else row_ids()
    last = ids == (0 if by == 1 else (127 if axis == 1 else 7))
    rolled_main, rolled_edge = roll(main, by, axis), roll(edge, by, axis)
    return jnp.where(last, rolled_edge, rolled_main), jnp.where(last, rolled_main, rolled_edge)


def merge(x, gates):
    lanes = lane_ids()
    for step, gate in zip((1, 2, 4), gates):
        other = jnp.take_along_axis(x, lanes ^ step, axis=1)
        x = x + jnp.where(gate, other, x)
    return x * 0.125


def inverse(c):
    m = [[c[0] + 1.0, c[1], c[2]], [c[3], c[4] + 1.0, c[5]], [c[6], c[7], c[8] + 1.0]]

    def cof(a, b):
        i, j, p, q = (a + 1) % 3, (a + 2) % 3, (b + 1) % 3, (b + 2) % 3
        return m[i][p] * m[j][q] - m[i][q] * m[j][p]

    cofs = [[cof(a, b) for b in range(3)] for a in range(3)]
    det = m[0][0] * cofs[0][0] + m[0][1] * cofs[0][1] + m[0][2] * cofs[0][2]
    inv = 1.0 / det
    return [cofs[b][a] * inv for a in range(3) for b in range(3)]


def row_tables(zf, zb, rows, total):
    factor = jnp.full((8, 128), zf[0], jnp.int32)
    for z in range(zb.shape[0]):
        factor = jnp.where(rows >= zb[z], zf[z + 1], factor)
    lat = ((rows.astype(jnp.float32) + 0.5) / total - 0.5) * jnp.pi
    metric = EAST / jnp.maximum(factor.astype(jnp.float32) * jnp.cos(lat), FLOOR)
    return metric, [factor > s for s in (1, 2, 4)]


def kernel(zf, zb, e_ref, h_ref, c_ref, eo_ref, ho_ref, rows_e, rows_h, rows_c, pack, got, got2, ee, hh, uu, mine, caps, sums,
           send, recv, cap_send, cap_recv, *, bands, lons):
    band, lon = lax.axis_index("band"), lax.axis_index("lon")
    at_south, at_north = band == 0, band == bands - 1
    north, south = band + 1, band - 1
    east, west = lax.rem(lon + 1, lons), lax.rem(lon + lons - 1, lons)
    pole = jnp.logical_or(at_south, at_north)

    barrier = pltpu.get_barrier_semaphore()

    def greet(b, l):
        pl.semaphore_signal(barrier, inc=1, device_id=(b, l), device_id_type=MESH)

    greet(band, east)
    greet(band, west)

    @pl.when(jnp.logical_not(at_north))
    def _():
        for l in (lon, east, west):
            greet(north, l)

    @pl.when(jnp.logical_not(at_south))
    def _():
        for l in (lon, east, west):
            greet(south, l)

    @pl.when(pole)
    def _():
        def one(d, _):
            greet(band, lax.rem(lon + d, lons))
            return 0
        lax.fori_loop(2, lons - 1, one, 0)

    lanes, rows = lane_ids(), row_ids()
    def pack_field(ref, first, count):
        def one(i, _):
            c, a = i // 2, lax.rem(i, 2)
            rolled = [roll(ref[c, a * 4 + q], 32 * q, 1) for q in range(4)]
            lo, hi = rolled[0], rolled[1]
            for q in range(1, 4):
                lo = jnp.where(lanes // 32 == q, rolled[q], lo)
                if q > 1:
                    hi = jnp.where(lanes // 32 == q - 1, rolled[q], hi)
            hi = jnp.where(lanes // 32 == 3, rolled[0], hi)
            pack[0, first * 2 + i] = lo
            pack[1, first * 2 + i] = hi
            return 0
        lax.fori_loop(0, count * 2, one, 0, unroll=3)

    pack_field(e_ref, 0, 3)
    pack_field(h_ref, 3, 3)
    pack_field(c_ref, 6, 9)

    @pl.when(pole)
    def _():
        pl.semaphore_wait(barrier, lons - 1 + 3)

    @pl.when(jnp.logical_not(pole))
    def _():
        pl.semaphore_wait(barrier, 8)

    def remote(src, dst, i, b, l):
        return pltpu.make_async_remote_copy(src_ref=src, dst_ref=dst, send_sem=send.at[i], recv_sem=recv.at[i],
                                            device_id=(b, l), device_id_type=MESH)

    def local(src, dst, i):
        return pltpu.make_async_copy(src, dst, recv.at[i])

    low, high = pl.ds(0, 4), pl.ds(4, 4)
    to_lon = [remote(pack.at[0], got.at[0], 0, band, west), remote(pack.at[1], got.at[1], 1, band, east)]
    to_north = [remote(pack.at[0, :, high], got2.at[0, :, high], 2, north, west),
                remote(pack.at[1, :, high], got2.at[1, :, high], 3, north, east)] + [
        remote(s.at[:, :, high], d.at[:, :, high], 4 + i, north, lon)
        for i, (s, d) in enumerate(((e_ref, rows_e), (h_ref, rows_h), (c_ref, rows_c)))]
    to_south = [remote(pack.at[0, :, low], got2.at[0, :, low], 7, south, west),
                remote(pack.at[1, :, low], got2.at[1, :, low], 8, south, east)] + [
        remote(s.at[:, :, low], d.at[:, :, low], 9 + i, south, lon)
        for i, (s, d) in enumerate(((e_ref, rows_e), (h_ref, rows_h), (c_ref, rows_c)))]
    own_high = [local(pack.at[0, :, high], got2.at[0, :, high], 2), local(pack.at[1, :, high], got2.at[1, :, high], 3)] + [
        local(s.at[:, :, high], d.at[:, :, high], 4 + i)
        for i, (s, d) in enumerate(((e_ref, rows_e), (h_ref, rows_h), (c_ref, rows_c)))]
    own_low = [local(pack.at[0, :, low], got2.at[0, :, low], 7), local(pack.at[1, :, low], got2.at[1, :, low], 8)] + [
        local(s.at[:, :, low], d.at[:, :, low], 9 + i)
        for i, (s, d) in enumerate(((e_ref, rows_e), (h_ref, rows_h), (c_ref, rows_c)))]
    for copy in to_lon:
        copy.start()

    @pl.when(jnp.logical_not(at_north))
    def _():
        for copy in to_north:
            copy.start()

    @pl.when(at_north)
    def _():
        for copy in own_low:
            copy.start()

    @pl.when(jnp.logical_not(at_south))
    def _():
        for copy in to_south:
            copy.start()

    @pl.when(at_south)
    def _():
        for copy in own_high:
            copy.start()

    metric, gates = [], []
    for block in range(2):
        shift = 0 if block == 0 else jnp.where(rows < 4, 8, -8)
        m, g = row_tables(zf, zb, band * 8 + rows + shift, 8 * bands)
        metric.append(m)
        gates.append(g)
    zero = jnp.zeros((8, 128), jnp.float32)
    for b in range(4):
        for c in range(3):
            ee[b, c, 8] = zero
            hh[b, c, 0] = zero

    def take_in(block, layer, load):
        for c in range(3):
            ee[block, c, layer] = load(c)
            hh[block, c, layer + 1] = load(3 + c)
        for i, value in enumerate(inverse([load(6 + c) for c in range(9)])):
            uu[block, i, layer] = value

    def own(k, _):
        take_in(0, k, lambda f: e_ref[f, k] if f < 3 else (h_ref[f - 3, k] if f < 6 else c_ref[f - 6, k]))
        return 0

    lax.fori_loop(0, 8, own, 0)

    def unpack(block, ref):
        def one(a, _):
            for q in range(4):
                take_in(block, a * 4 + q, lambda f: roll(
                    jnp.where(lanes // 32 == q, ref[0, 2 * f + a], ref[1, 2 * f + a]), -32 * q, 1))
            return 0
        lax.fori_loop(0, 2, one, 0)

    for copy in to_lon:
        copy.wait()
    unpack(1, got)

    @pl.when(jnp.logical_not(at_north))
    def _():
        for copy in to_north:
            copy.wait_send()
        for copy in to_south:
            copy.wait_recv()

    @pl.when(at_north)
    def _():
        for copy in own_low:
            copy.wait()

    @pl.when(jnp.logical_not(at_south))
    def _():
        for copy in to_south:
            copy.wait_send()
        for copy in to_north:
            copy.wait_recv()

    @pl.when(at_south)
    def _():
        for copy in own_high:
            copy.wait()

    def outer(k, _):
        take_in(2, k, lambda f: rows_e[f, k] if f < 3 else (rows_h[f - 3, k] if f < 6 else rows_c[f - 6, k]))
        return 0

    lax.fori_loop(0, 8, outer, 0)
    unpack(3, got2)

    def cap_means(step, read):
        for i in range(2):
            mine[step, i] = read(2 * i)

        def copy_to(d):
            return pltpu.make_async_remote_copy(src_ref=mine.at[step], dst_ref=caps.at[step, d - 1], send_sem=cap_send.at[step],
                                                recv_sem=cap_recv.at[step], device_id=(band, lax.rem(lon + d, lons)),
                                                device_id_type=MESH)

        def start(d, _):
            copy_to(d).start()
            return 0

        lax.fori_loop(1, lons, start, 0)
        pltpu.make_async_copy(caps.at[step], caps.at[step], cap_send.at[step]).wait()
        pltpu.make_async_copy(caps.at[step], caps.at[step], cap_recv.at[step]).wait()
        for i in range(2):
            total = mine[step, i] + jnp.sum(caps[step, :, i], axis=0)
            sums[i] = jnp.broadcast_to(jnp.sum(total, axis=1, keepdims=True) * (1.0 / (128 * lons)), (8, 128))

    def forward(k, _):
        f = [[ee[b, c, k] for b in range(4)] for c in range(3)]
        up = [[ee[b, c, k + 1] for b in range(4)] for c in range(2)]
        fe, fn = {}, {}
        for c in (1, 2):
            fe[c] = [*pair_shift(f[c][0], f[c][1], -1, 1), *pair_shift(f[c][2], f[c][3], -1, 1)]
        for c in (0, 2):
            a, b = pair_shift(f[c][0], f[c][2], -1, 0), pair_shift(f[c][1], f[c][3], -1, 0)
            ghost = jnp.broadcast_to(sums[c // 2, pl.ds(k, 1), :], (8, 128))
            cap = jnp.logical_and(rows == 7, at_north)
            fn[c] = [jnp.where(cap, ghost, a[0]), jnp.where(cap, ghost, b[0]), a[1], b[1]]
        for b in range(4):
            m, g = metric[b // 2], gates[b // 2]
            curl = (NORTH * (fn[2][b] - f[2][b]) - RADIAL * (up[1][b] - f[1][b]),
                    RADIAL * (up[0][b] - f[0][b]) - m * (fe[2][b] - f[2][b]),
                    m * (fe[1][b] - f[1][b]) - NORTH * (fn[0][b] - f[0][b]))
            for c in range(3):
                hh[b, c, k + 1] = merge(hh[b, c, k + 1] - curl[c], g)
        return 0

    def backward(k, _):
        f = [[hh[b, c, k + 1] for b in range(4)] for c in range(3)]
        down = [[hh[b, c, k] for b in range(4)] for c in range(2)]
        fw, fs = {}, {}
        for c in (1, 2):
            fw[c] = [*pair_shift(f[c][0], f[c][1], 1, 1), *pair_shift(f[c][2], f[c][3], 1, 1)]
        for c in (0, 2):
            a, b = pair_shift(f[c][0], f[c][2], 1, 0), pair_shift(f[c][1], f[c][3], 1, 0)
            ghost = jnp.broadcast_to(sums[c // 2, pl.ds(k, 1), :], (8, 128))
            cap = jnp.logical_and(rows == 0, at_south)
            fs[c] = [jnp.where(cap, ghost, a[0]), jnp.where(cap, ghost, b[0]), a[1], b[1]]
        for b in range(4):
            m, g = metric[b // 2], gates[b // 2]
            curl = (NORTH * (f[2][b] - fs[2][b]) - RADIAL * (f[1][b] - down[1][b]),
                    RADIAL * (f[0][b] - down[0][b]) - m * (f[2][b] - fw[2][b]),
                    m * (f[1][b] - fw[1][b]) - NORTH * (f[0][b] - fs[0][b]))
            old = [ee[b, c, k] for c in range(3)]
            drive = [2.0 * old[c] + curl[c] for c in range(3)]
            for a in range(3):
                new = uu[b, 3 * a, k] * drive[0] + uu[b, 3 * a + 1, k] * drive[1] + uu[b, 3 * a + 2, k] * drive[2] - old[a]
                ee[b, a, k] = merge(new, g)
        return 0

    def step(n, _):
        @pl.when(at_north)
        def _():
            cap_means(n, lambda c: ee[0, c, pl.ds(0, 8), 7, :])

        lax.fori_loop(0, 8, forward, 0)

        @pl.when(at_south)
        def _():
            cap_means(n, lambda c: hh[0, c, pl.ds(1, 8), 0, :])

        lax.fori_loop(0, 8, backward, 0)
        return 0

    lax.fori_loop(0, STEPS, step, 0)
    for c in range(3):
        eo_ref[c] = ee[0, c, pl.ds(0, 8)]
        ho_ref[c] = hh[0, c, pl.ds(1, 8)]


def solution(mesh):
    bands, lons = mesh.shape["band"], mesh.shape["lon"]

    def on_device(e, h, c, zone_factor, zone_bounds):
        vmem, smem = pl.BlockSpec(memory_space=pltpu.VMEM), pl.BlockSpec(memory_space=pltpu.SMEM)
        f32 = lambda *shape: pltpu.VMEM(shape, jnp.float32)
        like = jax.ShapeDtypeStruct(e.shape, e.dtype)
        return pl.pallas_call(
            functools.partial(kernel, bands=bands, lons=lons),
            out_shape=(like, like),
            in_specs=[smem, smem, vmem, vmem, vmem],
            out_specs=(vmem, vmem),
            scratch_shapes=[
                f32(3, 8, 8, 128), f32(3, 8, 8, 128), f32(9, 8, 8, 128),
                f32(2, 2 * FIELDS, 8, 128), f32(2, 2 * FIELDS, 8, 128), f32(2, 2 * FIELDS, 8, 128),
                f32(4, 3, 9, 8, 128), f32(4, 3, 9, 8, 128), f32(4, 9, 8, 8, 128),
                f32(STEPS, 2, 8, 128), f32(STEPS, lons - 1, 2, 8, 128), f32(2, 8, 128),
                pltpu.SemaphoreType.DMA((12,)), pltpu.SemaphoreType.DMA((12,)),
                pltpu.SemaphoreType.DMA((STEPS,)), pltpu.SemaphoreType.DMA((STEPS,)),
            ],
            compiler_params=pltpu.CompilerParams(collective_id=0, has_side_effects=True, vmem_limit_bytes=32 * 1024 * 1024),
        )(zone_factor, zone_bounds, e, h, c)

    spread = P(None, None, "band", "lon")
    return jax.shard_map(on_device, mesh=mesh, in_specs=(spread, spread, spread, P(), P()), out_specs=(spread, spread),
                         check_vma=False)
```

time: 1950 us -> 102 us (0.05)
  the two profiles are of different devices: /device:TPU:1 before, /device:TPU:6 now
where the time goes in v1:
time: 102 us; the launch traced here: 101 us
  Pallas kernels  95.5 us (94%)
  local copies, waits for them, and re-layouts  5.33 us (5%)
    pallas_call x1, Pallas kernels, on_device(): pl.pallas_call(functools.partial(kernel, bands=bands, lons=lons), out_sha...  95.5 us
    unnamed x12, local copies, waits for them, and re-layouts  5.33 us

profile of v1, /device:TPU:6, one launch (start us, length us, event | category | flops | bytes accessed | tf_op | source)
XLA Modules:
  0.0 101.5 jit_solution(16142584749975532101)
XLA Ops:
  0.6 0.0 copy-start
  0.6 1.0 copy-done
  1.6 0.0 copy-start.1
  1.6 0.9 copy-done.1
  2.5 0.0 copy-start.2
  2.5 0.9 copy-done.2
  3.4 0.0 copy-start.3
  3.4 0.7 copy-done.3
  4.0 0.0 copy-start.4
  4.0 0.7 copy-done.4
  4.7 95.5 %shard_map.68 = (f32[3,8,8,128]{3,2,1,0:T(8,128)S(1)}, f32[3,8,8,128]{3,2,1,0:T(8,128)S(1)}) custom-call(s32[8]{0:T(128)S(1)} %copy-done.3, s32[7]{0:T(128)S(1)} %copy-done.4, f32[3,8,8,128]{3,2,1,0:T(8,128)S(1)} %copy-done.1, f32[3,8,8,128]{3,2,1,0:T(8,128)S(1)} %copy-done.2, f32[9,8,8,128]{3,2,1,0:T(8,128)S(1)} %copy-done), custom_call_target="tpu_custom_call" | custom-call | tf_op jit(solution)/shard_map/pallas_call | solution.py:331
  100.2 0.6 copy.9
  100.8 0.6 copy.10
Async XLA Ops:
  0.6 1.0 copy-start
  1.6 0.9 copy-start.1
  2.5 0.9 copy-start.2
  3.4 0.7 copy-start.3
  4.0 0.7 copy-start.4

commit v2 on v1

v2 whole, which is shorter than its diff:
```python
import functools

import jax
import jax.numpy as jnp
from jax import lax
from jax.experimental import pallas as pl
from jax.experimental.pallas import tpu as pltpu
from jax.sharding import PartitionSpec as P

MESH = pl.DeviceIdType.MESH
STEPS = 4
NORTH, RADIAL, EAST, FLOOR = 0.45, 0.5, 0.12, 0.25
FIELDS = 15


def lane_ids():
    return lax.broadcasted_iota(jnp.int32, (8, 128), 1)


def row_ids():
    return lax.broadcasted_iota(jnp.int32, (8, 128), 0)


def roll(x, by, axis):
    by = by % x.shape[axis]
    return x if by == 0 else pltpu.roll(x, by, axis)


def pair_shift(main, edge, by, axis):
    ids = lane_ids() if axis == 1 else row_ids()
    last = ids == (0 if by == 1 else (127 if axis == 1 else 7))
    rolled_main, rolled_edge = roll(main, by, axis), roll(edge, by, axis)
    return jnp.where(last, rolled_edge, rolled_main), jnp.where(last, rolled_main, rolled_edge)


def merge(x, gates):
    lanes = lane_ids()
    for step, gate in zip((1, 2, 4), gates):
        other = jnp.take_along_axis(x, lanes ^ step, axis=1)
        x = x + jnp.where(gate, other, x)
    return x * 0.125


def inverse(c):
    m = [[c[0] + 1.0, c[1], c[2]], [c[3], c[4] + 1.0, c[5]], [c[6], c[7], c[8] + 1.0]]

    def cof(a, b):
        i, j, p, q = (a + 1) % 3, (a + 2) % 3, (b + 1) % 3, (b + 2) % 3
        return m[i][p] * m[j][q] - m[i][q] * m[j][p]

    cofs = [[cof(a, b) for b in range(3)] for a in range(3)]
    det = m[0][0] * cofs[0][0] + m[0][1] * cofs[0][1] + m[0][2] * cofs[0][2]
    inv = 1.0 / det
    return [cofs[b][a] * inv for a in range(3) for b in range(3)]


def row_tables(zf, zb, rows, total):
    factor = jnp.full((8, 128), zf[0], jnp.int32)
    for z in range(zb.shape[0]):
        factor = jnp.where(rows >= zb[z], zf[z + 1], factor)
    lat = ((rows.astype(jnp.float32) + 0.5) / total - 0.5) * jnp.pi
    metric = EAST / jnp.maximum(factor.astype(jnp.float32) * jnp.cos(lat), FLOOR)
    return metric, factor


def batched(fn, tiles):
    whole = fn(jnp.concatenate(tiles, axis=0))
    return [whole[8 * i : 8 * i + 8] for i in range(len(tiles))]


def total_of(terms):
    out = None
    for factor, tile in terms:
        if tile is None:
            continue
        if out is None:
            out = tile if isinstance(factor, float) and factor == 1.0 else factor * tile
        elif isinstance(factor, float) and factor == 1.0:
            out = out + tile
        elif isinstance(factor, float) and factor == -1.0:
            out = out - tile
        else:
            out = out + factor * tile
    return out


class PoleRows:
    def __init__(self, at_north, metric, gates):
        self.at_north, self.metric, self.gates = at_north, metric, gates

    def shift_layer(self, field, c, r, b, source, by):
        rows = row_ids()
        key = source if source == "free" else (source[0], source[1] + by)
        tile = field.get((c, r, b, key))
        if tile is None:
            return None
        return jnp.where(rows == (7 if by == 1 else 0), 0.0, pltpu.roll(tile, 7 if by == 1 else 1, 0))

    def turn(self, field, comps, by):
        ids = [i for i in field if i[0] in comps and i[2] == 0]
        if not ids:
            return {}
        edge = lane_ids() == (0 if by == 1 else 127)
        moved = batched(lambda x: pltpu.roll(x, by % 128, 1), [field[i[0], i[1], b, i[3]] for b in range(2) for i in ids])
        out = {}
        for n, i in enumerate(ids):
            main, other = moved[n], moved[n + len(ids)]
            out[i] = jnp.where(edge, other, main)
            out[i[0], i[1], 1, i[3]] = jnp.where(edge, main, other)
        return out

    def merge(self, field):
        ids = list(field)
        tiles = [field[i] for i in ids]
        for level, step in enumerate((1, 2, 4)):
            def swap(x):
                return jnp.take_along_axis(x, lax.broadcasted_iota(jnp.int32, x.shape, 1) ^ step, axis=1)
            others = batched(swap, tiles)
            tiles = [t + jnp.where(self.gates[i[1]][level], o, t) for i, t, o in zip(ids, tiles, others)]
        return {i: t * 0.125 for i, t in zip(ids, tiles)}

    def keys(self, field, spread, extra=()):
        found = []
        for source in [i[3] for i in field] + list(extra):
            for s in ([source] if source == "free" else [source, (source[0], source[1] + spread)]):
                if s not in found:
                    found.append(s)
        return found

    def forward(self, e, h, wanted, merged=True):
        ahead = -1 if self.at_north else 1
        fe = self.turn(e, (1, 2), -1)
        new = {}
        for source in self.keys(e, -1, [i[3] for i in h]):
            for c, r in wanted:
                for b in range(2):
                    m = self.metric[r]
                    up = lambda c: self.shift_layer(e, c, r, b, source, 1)
                    at = lambda c: e.get((c, r, b, source))
                    north = lambda c: e.get((c, r + ahead, b, source))
                    east = lambda c: fe.get((c, r, b, source))
                    if c == 0:
                        curl = [(-NORTH, north(2)), (NORTH, at(2)), (RADIAL, up(1)), (-RADIAL, at(1))]
                    elif c == 1:
                        curl = [(-RADIAL, up(0)), (RADIAL, at(0)), (m, east(2)), (-m, at(2))]
                    else:
                        curl = [(-m, east(1)), (m, at(1)), (NORTH, north(0)), (-NORTH, at(0))]
                    tile = total_of([(1.0, h.get((c, r, b, source)))] + curl)
                    if tile is not None:
                        new[c, r, b, source] = tile
        return self.merge(new) if merged else new

    def drive(self, e, h, rows):
        behind = 1 if self.at_north else -1
        fw = self.turn(h, (1, 2), 1)
        new = {}
        for source in self.keys(h, 1, [i[3] for i in e]):
            for r in rows:
                for b in range(2):
                    m = self.metric[r]
                    down = lambda c: self.shift_layer(h, c, r, b, source, -1)
                    at = lambda c: h.get((c, r, b, source))
                    south = lambda c: h.get((c, r + behind, b, source))
                    west = lambda c: fw.get((c, r, b, source))
                    curls = ([(NORTH, at(2)), (-NORTH, south(2)), (-RADIAL, at(1)), (RADIAL, down(1))],
                             [(RADIAL, at(0)), (-RADIAL, down(0)), (-m, at(2)), (m, west(2))],
                             [(m, at(1)), (-m, west(1)), (-NORTH, at(0)), (NORTH, south(0))])
                    for c in range(3):
                        tile = total_of([(2.0, e.get((c, r, b, source)))] + curls[c])
                        if tile is not None:
                            new[c, r, b, source] = tile
        return new

    def update(self, u, drive, e, wanted, merged=True):
        new = {}
        for source in self.keys(drive, 0, [i[3] for i in e]):
            for a, r in wanted:
                for b in range(2):
                    tile = total_of([(u[3 * a + c, r, b], drive.get((c, r, b, source))) for c in range(3)]
                                    + [(-1.0, e.get((a, r, b, source)))])
                    if tile is not None:
                        new[a, r, b, source] = tile
        return self.merge(new) if merged else new


def every(rows):
    return [(c, r) for r in rows for c in range(3)]


def only(field, source):
    return {i: t for i, t in field.items() if (i[3] == "free") == source}


def pole_chain(at_north, load_e, load_h, load_u, metric, gates):
    p = PoleRows(at_north, metric, gates)
    deep = range(4) if at_north else range(5)
    e = {(c, r, b, "free"): load_e(c, r, b) for c in range(3) for r in deep for b in range(2)}
    h = {(c, r, b, "free"): load_h(c, r, b) for c in range(3) for r in range(4) for b in range(2)}
    u = {(i, r, b): load_u(i, r, b) for i in range(9) for r in range(3 if at_north else 4) for b in range(2)}
    out = {}

    def note(n, field, initial=False):
        for (c, r, b, source), tile in field.items():
            if r == 0 and b == 0 and c != 1:
                out[("free", n) if source == "free" else ("response", n) + source, c] = tile

    unit = jnp.ones((8, 128), jnp.float32)
    ends = [(0, 0), (2, 0)]
    if at_north:
        note(0, e)
        h = p.forward(e, h, every(range(4)))
        for b in range(2):
            h[0, 0, b, (2, 0)] = -NORTH * unit
            h[2, 0, b, (0, 0)] = NORTH * unit
        def back(e, h, free_rows, rows, wanted=None, merged=True):
            new = {}
            for free, rr in ((True, free_rows), (False, rows)):
                ee, hh = only(e, free), only(h, free)
                d = p.drive(ee, hh, rr)
                new.update({(i, free): t for i, t in d.items()})
            drive = {i: t for (i, _), t in new.items()}
            want = wanted or every(sorted(set(free_rows) | set(rows)))
            return p.update(u, drive, {i: t for i, t in e.items() if (i[1] in (free_rows if i[3] == "free" else rows))}, want, merged)

        e = back(e, h, range(3), range(1))
        note(1, e)
        h = p.forward(e, h, every(range(3)))
        h = {i: t for i, t in h.items() if i[3] == "free" or i[1] < 2}
        e = back(e, h, range(2), range(2))
        note(2, e)
        h = p.forward(e, h, every(range(2)))
        e = back(e, h, range(1), range(1), ends, False)
        note(3, e)
    else:
        h = p.forward(e, h, every(range(4)))
        note(0, h)
        drive = p.drive(e, h, range(4))
        for b in range(2):
            drive[0, 0, b, (2, 0)] = -NORTH * unit
            drive[2, 0, b, (0, 0)] = NORTH * unit
        e = p.update(u, drive, {i: t for i, t in e.items() if i[1] < 4}, every(range(4)))
        h = p.forward(e, {i: t for i, t in h.items() if i[1] < 3}, every(range(3)))
        note(1, h)
        drive = p.drive(e, h, range(3))
        e = p.update(u, drive, {i: t for i, t in e.items() if i[1] < 3}, every(range(3)))
        h = p.forward(e, {i: t for i, t in h.items() if i[1] < 2}, every(range(2)))
        note(2, h)
        drive = p.drive(e, h, range(2))
        e = p.update(u, drive, {i: t for i, t in e.items() if i[1] < 2}, every(range(2)))
        h = p.forward(e, {i: t for i, t in h.items() if i[1] < 1}, ends, False)
        note(3, h)
    return out


def columns(tiles):
    lanes = lane_ids()
    count = 128
    tiles = tiles + [None] * (count - len(tiles))
    while count > 1:
        count //= 2
        first, second = tiles[:count], tiles[count:]
        low = (lanes & count) == 0
        zero = jnp.zeros((8, 128), jnp.float32)
        pairs = [(a, b) for a, b in zip(first, second) if a is not None]
        give = [jnp.where(low, zero if b is None else b, a) for a, b in pairs]
        take = [jnp.where(low, a, zero if b is None else b) for a, b in pairs]
        swapped = batched(lambda x: jnp.take_along_axis(x, lax.broadcasted_iota(jnp.int32, x.shape, 1) ^ count, axis=1), give)
        tiles = [t + s for t, s in zip(take, swapped)]
        tiles = tiles + [None] * (count - len(tiles))
    return tiles[0]


def solve_caps(names, total):
    rows = row_ids()
    spread = dict(zip(names, batched(lambda x: x, [jnp.take_along_axis(total, jnp.full((8, 128), q, jnp.int32), axis=1)
                                                   for q in range(len(names))])))
    caps = []

    def moved(tile, d):
        if d == 0:
            return tile
        kept = rows >= d if d > 0 else rows < 8 + d
        return jnp.where(kept, pltpu.roll(tile, d % 8, 0), 0.0)

    for n in range(STEPS):
        value = {c: spread[("free", n), c] for c in (0, 2)}
        for m in range(n):
            shifted = {}
            for name, c in names:
                if name[0] == "response" and name[1] == n - m:
                    if name[2:] not in shifted:
                        shifted[name[2:]] = moved(caps[m][name[2]], name[3])
                    value[c] = value[c] + spread[name, c] * shifted[name[2:]]
        caps.append(value)
    return caps


def kernel(zf, zb, e_in, h_in, c_in, eo_ref, ho_ref, e_ref, h_ref, c_ref, rows_e, rows_h, rows_c, pack, got, got2, ee, hh, uu, mine,
           caps, sums, load_sem, send, recv, cap_send, cap_recv, *, bands, lons):
    band, lon = lax.axis_index("band"), lax.axis_index("lon")
    at_south, at_north = band == 0, band == bands - 1
    inner_north, inner_south = jnp.logical_not(at_north), jnp.logical_not(at_south)
    north, south = band + 1, band - 1
    east, west = lax.rem(lon + 1, lons), lax.rem(lon + lons - 1, lons)
    pole = jnp.logical_or(at_south, at_north)

    loads = [pltpu.make_async_copy(s, d, load_sem.at[i]) for i, (s, d) in enumerate(((e_in, e_ref), (h_in, h_ref), (c_in, c_ref)))]
    for load in loads:
        load.start()

    barrier = pltpu.get_barrier_semaphore()

    def greet(b, l):
        pl.semaphore_signal(barrier, inc=1, device_id=(b, l), device_id_type=MESH)

    greet(band, east)
    greet(band, west)

    @pl.when(inner_north)
    def _():
        for l in (east, west, lon):
            greet(north, l)

    @pl.when(inner_south)
    def _():
        for l in (east, west, lon):
            greet(south, l)

    @pl.when(pole)
    def _():
        def one(d, _):
            greet(band, lax.rem(lon + d, lons))
            return 0
        lax.fori_loop(2, lons - 1, one, 0)

    lanes, rows = lane_ids(), row_ids()

    def pack_field(ref, first, count):
        def one(i, _):
            tiles = [(c, a) for c in range(3) for a in range(2)]
            rolled = [[roll(ref[i * 3 + c, a * 4 + q], 32 * q, 1) for q in range(4)] for c, a in tiles]
            for n, t in enumerate(rolled):
                lo, hi = t[0], t[1]
                for q in range(1, 4):
                    lo = jnp.where(lanes // 32 == q, t[q], lo)
                    if q > 1:
                        hi = jnp.where(lanes // 32 == q - 1, t[q], hi)
                hi = jnp.where(lanes // 32 == 3, t[0], hi)
                pack[0, first * 2 + i * 6 + n] = lo
                pack[1, first * 2 + i * 6 + n] = hi
            return 0
        if count == 3:
            one(0, 0)
        else:
            lax.fori_loop(0, count // 3, one, 0)

    def remote(src, dst, i, b, l):
        return pltpu.make_async_remote_copy(src_ref=src, dst_ref=dst, send_sem=send.at[i], recv_sem=recv.at[i],
                                            device_id=(b, l), device_id_type=MESH)

    fields, conduct = pl.ds(0, 12), pl.ds(12, 18)
    to_lon = [[remote(pack.at[k, part], got.at[k, part], 2 * n + k, band, (west, east)[k]) for k in range(2)]
              for n, part in enumerate((fields, conduct))]
    to_north = [[remote(pack.at[k, part, pl.ds(8 - d[k], d[k])], got2.at[k, part, pl.ds(8 - d[k], d[k])], 4 + 2 * n + k, north, (west, east)[k])
                 for k in range(2)] for n, (part, d) in enumerate(((fields, (4, 3)), (conduct, (3, 2))))]
    to_south = [[remote(pack.at[k, part, pl.ds(0, d[k])], got2.at[k, part, pl.ds(0, d[k])], 8 + 2 * n + k, south, (west, east)[k])
                 for k in range(2)] for n, (part, d) in enumerate(((fields, (3, 4)), (conduct, (2, 3))))]
    trio = ((e_ref, rows_e), (h_ref, rows_h), (c_ref, rows_c))
    rows_north = [remote(s.at[:, :, pl.ds(8 - d, d)], t.at[:, :, pl.ds(8 - d, d)], 12 + i, north, lon)
                  for i, ((s, t), d) in enumerate(zip(trio, (4, 4, 3)))]
    rows_south = [remote(s.at[:, :, pl.ds(0, d)], t.at[:, :, pl.ds(0, d)], 15 + i, south, lon)
                  for i, ((s, t), d) in enumerate(zip(trio, (4, 3, 3)))]

    def send_part(n):
        for copy in to_lon[n]:
            copy.start()

        @pl.when(inner_north)
        def _():
            for copy in to_north[n] + (rows_north[:2] if n == 0 else rows_north[2:]):
                copy.start()

        @pl.when(inner_south)
        def _():
            for copy in to_south[n] + (rows_south[:2] if n == 0 else rows_south[2:]):
                copy.start()

    loads[0].wait()
    loads[1].wait()
    pack_field(e_ref, 0, 3)
    pack_field(h_ref, 3, 3)

    @pl.when(pole)
    def _():
        pl.semaphore_wait(barrier, lons - 1 + 3)

    @pl.when(jnp.logical_not(pole))
    def _():
        pl.semaphore_wait(barrier, 8)

    send_part(0)
    loads[2].wait()
    pack_field(c_ref, 6, 9)
    send_part(1)

    metric, factors, gates = [], [], []
    for block in range(2):
        shift = 0 if block == 0 else jnp.where(rows < 4, 8, -8)
        m, f = row_tables(zf, zb, band * 8 + rows + shift, 8 * bands)
        metric.append(m)
        factors.append(f)
        gates.append([f > s for s in (1, 2, 4)])
    zero = jnp.zeros((8, 128), jnp.float32)
    for b in range(4):
        for c in range(3):
            ee[b, c, 8] = zero
            hh[b, c, 0] = zero
    for n in range(STEPS):
        for i in range(2):
            sums[n, i] = zero

    def take_in(block, layer, load):
        for c in range(3):
            ee[block, c, layer] = load(c)
            hh[block, c, layer + 1] = load(3 + c)
        for i, value in enumerate(inverse([load(6 + c) for c in range(9)])):
            uu[block, i, layer] = value

    def own(k, _):
        take_in(0, k, lambda f: e_ref[f, k] if f < 3 else (h_ref[f - 3, k] if f < 6 else c_ref[f - 6, k]))
        return 0

    lax.fori_loop(0, 8, own, 0)

    def unpack(block, ref):
        def one(a, _):
            for q in range(4):
                tiles = [roll(jnp.where(lanes // 32 == q, ref[0, 2 * f + a], ref[1, 2 * f + a]), -32 * q, 1) for f in range(FIELDS)]
                take_in(block, a * 4 + q, lambda f: tiles[f])
            return 0
        lax.fori_loop(0, 2, one, 0)

    for n in range(2):
        for copy in to_lon[n]:
            copy.wait_recv()
    unpack(1, got)

    offsets = sorted(((i // 32, i // 8 % 4, i % 8) for i in range(1, 64)),
                     key=lambda o: -(4 * o[0] + min(o[1], 4 - o[1]) + min(o[2], 8 - o[2])))

    def cap_copy(n, offset):
        hi, x, z = lon // 32, lax.rem(lon // 8, 4), lax.rem(lon, 8)
        target = lax.rem(hi + offset[0], 2) * 32 + lax.rem(x + offset[1], 4) * 8 + lax.rem(z + offset[2], 8)
        return pltpu.make_async_remote_copy(src_ref=mine, dst_ref=caps.at[n], send_sem=cap_send.at[0], recv_sem=cap_recv.at[0],
                                            device_id=(band, target), device_id_type=MESH)

    names = {}
    for name, is_north, condition in (("north", True, at_north), ("south", False, at_south)):
        @pl.when(condition)
        def _():
            def sub(r):
                return 7 - r if is_north else r
            m = [jnp.broadcast_to(metric[0][sub(r) : sub(r) + 1, :], (8, 128)) for r in range(5)]
            f = [jnp.broadcast_to(factors[0][sub(r) : sub(r) + 1, :], (8, 128)) for r in range(5)]
            found = pole_chain(is_north, lambda c, r, b: ee[b, c, pl.ds(0, 8), sub(r), :], lambda c, r, b: hh[b, c, pl.ds(1, 8), sub(r), :],
                               lambda i, r, b: uu[b, i, pl.ds(0, 8), sub(r), :], m, [[x > s for s in (1, 2, 4)] for x in f])
            names[name] = list(found)
            mine[...] = columns(list(found.values()))

    @pl.when(pole)
    def _():
        for n, offset in enumerate(offsets):
            cap_copy(n, offset).start()

    @pl.when(inner_north)
    def _():
        for n in range(2):
            for copy in to_south[n]:
                copy.wait_recv()
        for copy in rows_south:
            copy.wait_recv()

    @pl.when(inner_south)
    def _():
        for n in range(2):
            for copy in to_north[n]:
                copy.wait_recv()
        for copy in rows_north:
            copy.wait_recv()

    def outer(k, _):
        take_in(2, k, lambda f: rows_e[f, k] if f < 3 else (rows_h[f - 3, k] if f < 6 else rows_c[f - 6, k]))
        return 0

    lax.fori_loop(0, 8, outer, 0)
    unpack(3, got2)

    @pl.when(pole)
    def _():
        pltpu.make_async_copy(caps, caps, cap_recv.at[0]).wait()

    for name, condition in (("north", at_north), ("south", at_south)):
        @pl.when(condition)
        def _():
            total = (mine[...] + jnp.sum(caps[...], axis=0)) * (1.0 / (128 * lons))
            for n, value in enumerate(solve_caps(names[name], total)):
                sums[n, 0] = value[0]
                sums[n, 1] = value[2]

    lane3 = lax.broadcasted_iota(jnp.int32, (8, 8, 128), 2)
    row3 = lax.broadcasted_iota(jnp.int32, (8, 8, 128), 1)
    metric3 = [jnp.broadcast_to(m, (8, 8, 128)) for m in metric]
    gates3 = [[jnp.broadcast_to(g, (8, 8, 128)).reshape(64, 128) for g in gs] for gs in gates]
    lane2 = lax.broadcasted_iota(jnp.int32, (64, 128), 1)

    def turn(f, by, axis):
        size = 128 if axis == 2 else 8
        seam = (lane3 if axis == 2 else row3) == (0 if by == 1 else size - 1)
        moved = [pltpu.roll(x.reshape(64, 128), by % 128, 1).reshape(8, 8, 128) if axis == 2 else pltpu.roll(x, by % 8, 1) for x in f]
        other = (1, 0, 3, 2) if axis == 2 else (2, 3, 0, 1)
        return [jnp.where(seam, moved[other[b]], moved[b]) for b in range(4)]

    def merge_all(f, store):
        x = {(b, c): f[b][c].reshape(64, 128) for b in range(4) for c in range(3)}
        for level, step in enumerate((1, 2, 4)):
            other = {i: jnp.take_along_axis(v, lane2 ^ step, axis=1) for i, v in x.items()}
            x = {(b, c): v + jnp.where(gates3[b // 2][level], other[b, c], v) for (b, c), v in x.items()}
        for (b, c), v in x.items():
            store(b, c, (v * 0.125).reshape(8, 8, 128))

    def ghost(n, c):
        return jnp.concatenate([jnp.broadcast_to(sums[n, c // 2, k : k + 1, :].reshape(1, 1, 128), (1, 8, 128)) for k in range(8)])

    def forward(n):
        f = [[ee[b, c, 0:8] for b in range(4)] for c in range(3)]
        up = [[ee[b, c, 1:9] for b in range(4)] for c in range(2)]
        fe = {c: turn(f[c], -1, 2) for c in (1, 2)}
        fn = {c: turn(f[c], -1, 1) for c in (0, 2)}
        cap = jnp.logical_and(row3 == 7, at_north)
        for c in (0, 2):
            value = ghost(n, c)
            for b in range(2):
                fn[c][b] = jnp.where(cap, value, fn[c][b])
        new = []
        for b in range(4):
            m = metric3[b // 2]
            curl = (NORTH * (fn[2][b] - f[2][b]) - RADIAL * (up[1][b] - f[1][b]),
                    RADIAL * (up[0][b] - f[0][b]) - m * (fe[2][b] - f[2][b]),
                    m * (fe[1][b] - f[1][b]) - NORTH * (fn[0][b] - f[0][b]))
            new.append([hh[b, c, 1:9] - curl[c] for c in range(3)])

        def store(b, c, v):
            hh[b, c, 1:9] = v

        merge_all(new, store)

    def backward(n):
        f = [[hh[b, c, 1:9] for b in range(4)] for c in range(3)]
        down = [[hh[b, c, 0:8] for b in range(4)] for c in range(2)]
        fw = {c: turn(f[c], 1, 2) for c in (1, 2)}
        fs = {c: turn(f[c], 1, 1) for c in (0, 2)}
        cap = jnp.logical_and(row3 == 0, at_south)
        for c in (0, 2):
            value = ghost(n, c)
            for b in range(2):
                fs[c][b] = jnp.where(cap, value, fs[c][b])
        new = []
        for b in range(4):
            m = metric3[b // 2]
            curl = (NORTH * (f[2][b] - fs[2][b]) - RADIAL * (f[1][b] - down[1][b]),
                    RADIAL * (f[0][b] - down[0][b]) - m * (f[2][b] - fw[2][b]),
                    m * (f[1][b] - fw[1][b]) - NORTH * (f[0][b] - fs[0][b]))
            old = [ee[b, c, 0:8] for c in range(3)]
            drive = [2.0 * old[c] + curl[c] for c in range(3)]
            new.append([uu[b, 3 * a, 0:8] * drive[0] + uu[b, 3 * a + 1, 0:8] * drive[1] + uu[b, 3 * a + 2, 0:8] * drive[2] - old[a]
                        for a in range(3)])

        def store(b, c, v):
            ee[b, c, 0:8] = v

        merge_all(new, store)

    def step(n, _):
        forward(n)
        backward(n)
        return 0

    lax.fori_loop(0, STEPS, step, 0)
    for c in range(3):
        eo_ref[c] = ee[0, c, pl.ds(0, 8)]
        ho_ref[c] = hh[0, c, pl.ds(1, 8)]

    for n in range(2):
        for copy in to_lon[n]:
            copy.wait_send()

    @pl.when(inner_north)
    def _():
        for copy in to_north[0] + to_north[1] + rows_north:
            copy.wait_send()

    @pl.when(inner_south)
    def _():
        for copy in to_south[0] + to_south[1] + rows_south:
            copy.wait_send()

    @pl.when(pole)
    def _():
        pltpu.make_async_copy(caps, caps, cap_send.at[0]).wait()


def solution(mesh):
    bands, lons = mesh.shape["band"], mesh.shape["lon"]

    def on_device(e, h, c, zone_factor, zone_bounds):
        vmem, smem, hbm = (pl.BlockSpec(memory_space=m) for m in (pltpu.VMEM, pltpu.SMEM, pl.ANY))
        f32 = lambda *shape: pltpu.VMEM(shape, jnp.float32)
        like = jax.ShapeDtypeStruct(e.shape, e.dtype)
        return pl.pallas_call(
            functools.partial(kernel, bands=bands, lons=lons),
            out_shape=(like, like),
            in_specs=[smem, smem, hbm, hbm, hbm],
            out_specs=(vmem, vmem),
            scratch_shapes=[
                f32(3, 8, 8, 128), f32(3, 8, 8, 128), f32(9, 8, 8, 128),
                f32(3, 8, 8, 128), f32(3, 8, 8, 128), f32(9, 8, 8, 128),
                f32(2, 2 * FIELDS, 8, 128), f32(2, 2 * FIELDS, 8, 128), f32(2, 2 * FIELDS, 8, 128),
                f32(4, 3, 9, 8, 128), f32(4, 3, 9, 8, 128), f32(4, 9, 8, 8, 128),
                f32(8, 128), f32(lons - 1, 8, 128), f32(STEPS, 2, 8, 128),
                pltpu.SemaphoreType.DMA((3,)), pltpu.SemaphoreType.DMA((18,)), pltpu.SemaphoreType.DMA((18,)),
                pltpu.SemaphoreType.DMA((1,)), pltpu.SemaphoreType.DMA((1,)),
            ],
            compiler_params=pltpu.CompilerParams(collective_id=0, has_side_effects=True, vmem_limit_bytes=32 * 1024 * 1024),
        )(zone_factor, zone_bounds, e, h, c)

    spread = P(None, None, "band", "lon")
    return jax.shard_map(on_device, mesh=mesh, in_specs=(spread, spread, spread, P(), P()), out_specs=(spread, spread),
                         check_vma=False)
```

time: 102 us -> 51.5 us (0.50)
  the two profiles are of different devices: /device:TPU:6 before, /device:TPU:2 now
where the time goes in v2:
time: 51.5 us; the launch traced here: 51.3 us
  Pallas kernels  45.3 us (88%)
  local copies, waits for them, and re-layouts  5.33 us (10%)
  between operations  0.65 us (1%)
    pallas_call x1, Pallas kernels, on_device(): pl.pallas_call(functools.partial(kernel, bands=bands, lons=lons), out_sha...  45.3 us
    unnamed x12, local copies, waits for them, and re-layouts  5.33 us

profile of v2, /device:TPU:2, one launch (start us, length us, event | category | flops | bytes accessed | tf_op | source)
XLA Modules:
  0.0 51.3 jit_solution(10538740623436663752)
XLA Ops:
  0.6 0.0 copy-start
  0.6 1.0 %copy-done = f32[9,8,8,128]{3,2,1,0:T(8,128)S(1)} copy-done((f32[9,8,8,128]{3,2,1,0:T(8,128)S(1)}, f32[9,8,8,128]{3,2,1,0:T(8,128)}, u32[]{:S(2)}) %copy-start) | copy-done | bytes 294936
  1.6 0.0 copy-start.1
  1.6 0.9 %copy-done.1 = f32[3,8,8,128]{3,2,1,0:T(8,128)S(1)} copy-done((f32[3,8,8,128]{3,2,1,0:T(8,128)S(1)}, f32[3,8,8,128]{3,2,1,0:T(8,128)}, u32[]{:S(2)}) %copy-start.1) | copy-done | bytes 98328
  2.5 0.0 copy-start.2
  2.5 0.9 %copy-done.2 = f32[3,8,8,128]{3,2,1,0:T(8,128)S(1)} copy-done((f32[3,8,8,128]{3,2,1,0:T(8,128)S(1)}, f32[3,8,8,128]{3,2,1,0:T(8,128)}, u32[]{:S(2)}) %copy-start.2) | copy-done | bytes 98328
  3.4 0.0 copy-start.3
  3.4 0.7 %copy-done.3 = s32[8]{0:T(128)S(1)} copy-done((s32[8]{0:T(128)S(1)}, s32[8]{0:T(128)}, u32[]{:S(2)}) %copy-start.3) | copy-done | bytes 56
  4.0 0.0 copy-start.4
  4.0 0.7 %copy-done.4 = s32[7]{0:T(128)S(1)} copy-done((s32[7]{0:T(128)S(1)}, s32[7]{0:T(128)}, u32[]{:S(2)}) %copy-start.4) | copy-done | bytes 52
  4.7 45.3 %shard_map.68 = (f32[3,8,8,128]{3,2,1,0:T(8,128)S(1)}, f32[3,8,8,128]{3,2,1,0:T(8,128)S(1)}) custom-call(s32[8]{0:T(128)S(1)} %copy-done.3, s32[7]{0:T(128)S(1)} %copy-done.4, f32[3,8,8,128]{3,2,1,0:T(8,128)S(1)} %copy-done.1, f32[3,8,8,128]{3,2,1,0:T(8,128)S(1)} %copy-done.2, f32[9,8,8,128]{3,2,1,0:T(8,128)S(1)} %copy-done), custom_call_target="tpu_custom_call" | custom-call | tf_op jit(solution)/shard_map/pallas_call | solution.py:619
  50.0 0.6 %copy.9 = f32[3,8,8,128]{3,2,1,0:T(8,128)} copy(f32[3,8,8,128]{3,2,1,0:T(8,128)S(1)} %get-tuple-element.4) | data formatting | bytes 196608
  50.6 0.6 %copy.10 = f32[3,8,8,128]{3,2,1,0:T(8,128)} copy(f32[3,8,8,128]{3,2,1,0:T(8,128)S(1)} %get-tuple-element.5) | data formatting | bytes 196608
Async XLA Ops:
  0.6 1.0 %copy-start = (f32[9,8,8,128]{3,2,1,0:T(8,128)S(1)}, f32[9,8,8,128]{3,2,1,0:T(8,128)}, u32[]{:S(2)}) copy-start(f32[9,8,8,128]{3,2,1,0:T(8,128)} %c_in.1) | copy-start | bytes 884740
  1.6 0.9 %copy-start.1 = (f32[3,8,8,128]{3,2,1,0:T(8,128)S(1)}, f32[3,8,8,128]{3,2,1,0:T(8,128)}, u32[]{:S(2)}) copy-start(f32[3,8,8,128]{3,2,1,0:T(8,128)} %e_in.1) | copy-start | bytes 294916
  2.5 0.9 %copy-start.2 = (f32[3,8,8,128]{3,2,1,0:T(8,128)S(1)}, f32[3,8,8,128]{3,2,1,0:T(8,128)}, u32[]{:S(2)}) copy-start(f32[3,8,8,128]{3,2,1,0:T(8,128)} %h_in.1) | copy-start | bytes 294916
  3.4 0.7 %copy-start.3 = (s32[8]{0:T(128)S(1)}, s32[8]{0:T(128)}, u32[]{:S(2)}) copy-start(s32[8]{0:T(128)} %zf.1) | copy-start | bytes 100
  4.0 0.7 %copy-start.4 = (s32[7]{0:T(128)S(1)}, s32[7]{0:T(128)}, u32[]{:S(2)}) copy-start(s32[7]{0:T(128)} %zb.1) | copy-start | bytes 88

commit v3 on v2

--- a/solution.py
+++ b/solution.py
@@ -88,26 +88,17 @@
     def __init__(self, at_north, metric, gates):
         self.at_north, self.metric, self.gates = at_north, metric, gates
 
-    def shift_layer(self, field, c, r, b, source, by):
+    def shift_layer(self, field, c, r, source, by):
         rows = row_ids()
         key = source if source == "free" else (source[0], source[1] + by)
-        tile = field.get((c, r, b, key))
+        tile = field.get((c, r, key))
         if tile is None:
             return None
         return jnp.where(rows == (7 if by == 1 else 0), 0.0, pltpu.roll(tile, 7 if by == 1 else 1, 0))
 
     def turn(self, field, comps, by):
-        ids = [i for i in field if i[0] in comps and i[2] == 0]
-        if not ids:
-            return {}
-        edge = lane_ids() == (0 if by == 1 else 127)
-        moved = batched(lambda x: pltpu.roll(x, by % 128, 1), [field[i[0], i[1], b, i[3]] for b in range(2) for i in ids])
-        out = {}
-        for n, i in enumerate(ids):
-            main, other = moved[n], moved[n + len(ids)]
-            out[i] = jnp.where(edge, other, main)
-            out[i[0], i[1], 1, i[3]] = jnp.where(edge, main, other)
-        return out
+        ids = [i for i in field if i[0] in comps]
+        return dict(zip(ids, batched(lambda x: pltpu.roll(x, by % 128, 1), [field[i] for i in ids]))) if ids else {}
 
     def merge(self, field):
         ids = list(field)
@@ -121,7 +112,7 @@
 
     def keys(self, field, spread, extra=()):
         found = []
-        for source in [i[3] for i in field] + list(extra):
+        for source in [i[2] for i in field] + list(extra):
             for s in ([source] if source == "free" else [source, (source[0], source[1] + spread)]):
                 if s not in found:
                     found.append(s)
@@ -131,55 +122,52 @@
         ahead = -1 if self.at_north else 1
         fe = self.turn(e, (1, 2), -1)
         new = {}
-        for source in self.keys(e, -1, [i[3] for i in h]):
+        for source in self.keys(e, -1, [i[2] for i in h]):
             for c, r in wanted:
-                for b in range(2):
-                    m = self.metric[r]
-                    up = lambda c: self.shift_layer(e, c, r, b, source, 1)
-                    at = lambda c: e.get((c, r, b, source))
-                    north = lambda c: e.get((c, r + ahead, b, source))
-                    east = lambda c: fe.get((c, r, b, source))
-                    if c == 0:
-                        curl = [(-NORTH, north(2)), (NORTH, at(2)), (RADIAL, up(1)), (-RADIAL, at(1))]
-                    elif c == 1:
-                        curl = [(-RADIAL, up(0)), (RADIAL, at(0)), (m, east(2)), (-m, at(2))]
-                    else:
-                        curl = [(-m, east(1)), (m, at(1)), (NORTH, north(0)), (-NORTH, at(0))]
-                    tile = total_of([(1.0, h.get((c, r, b, source)))] + curl)
-                    if tile is not None:
-                        new[c, r, b, source] = tile
+                m = self.metric[r]
+                up = lambda c: self.shift_layer(e, c, r, source, 1)
+                at = lambda c: e.get((c, r, source))
+                north = lambda c: e.get((c, r + ahead, source))
+                east = lambda c: fe.get((c, r, source))
+                if c == 0:
+                    curl = [(-NORTH, north(2)), (NORTH, at(2)), (RADIAL, up(1)), (-RADIAL, at(1))]
+                elif c == 1:
+                    curl = [(-RADIAL, up(0)), (RADIAL, at(0)), (m, east(2)), (-m, at(2))]
+                else:
+                    curl = [(-m, east(1)), (m, at(1)), (NORTH, north(0)), (-NORTH, at(0))]
+                tile = total_of([(1.0, h.get((c, r, source)))] + curl)
+                if tile is not None:
+                    new[c, r, source] = tile
         return self.merge(new) if merged else new
 
     def drive(self, e, h, rows):
         behind = 1 if self.at_north else -1
         fw = self.turn(h, (1, 2), 1)
         new = {}
-        for source in self.keys(h, 1, [i[3] for i in e]):
+        for source in self.keys(h, 1, [i[2] for i in e]):
             for r in rows:
-                for b in range(2):
-                    m = self.metric[r]
-                    down = lambda c: self.shift_layer(h, c, r, b, source, -1)
-                    at = lambda c: h.get((c, r, b, source))
-                    south = lambda c: h.get((c, r + behind, b, source))
-                    west = lambda c: fw.get((c, r, b, source))
-                    curls = ([(NORTH, at(2)), (-NORTH, south(2)), (-RADIAL, at(1)), (RADIAL, down(1))],
-                             [(RADIAL, at(0)), (-RADIAL, down(0)), (-m, at(2)), (m, west(2))],
-                             [(m, at(1)), (-m, west(1)), (-NORTH, at(0)), (NORTH, south(0))])
-                    for c in range(3):
-                        tile = total_of([(2.0, e.get((c, r, b, source)))] + curls[c])
-                        if tile is not None:
-                            new[c, r, b, source] = tile
+                m = self.metric[r]
+                down = lambda c: self.shift_layer(h, c, r, source, -1)
+                at = lambda c: h.get((c, r, source))
+                south = lambda c: h.get((c, r + behind, source))
+                west = lambda c: fw.get((c, r, source))
+                curls = ([(NORTH, at(2)), (-NORTH, south(2)), (-RADIAL, at(1)), (RADIAL, down(1))],
+                         [(RADIAL, at(0)), (-RADIAL, down(0)), (-m, at(2)), (m, west(2))],
+                         [(m, at(1)), (-m, west(1)), (-NORTH, at(0)), (NORTH, south(0))])
+                for c in range(3):
+                    tile = total_of([(2.0, e.get((c, r, source)))] + curls[c])
+                    if tile is not None:
+                        new[c, r, source] = tile
         return new
 
     def update(self, u, drive, e, wanted, merged=True):
         new = {}
-        for source in self.keys(drive, 0, [i[3] for i in e]):
+        for source in self.keys(drive, 0, [i[2] for i in e]):
             for a, r in wanted:
-                for b in range(2):
-                    tile = total_of([(u[3 * a + c, r, b], drive.get((c, r, b, source))) for c in range(3)]
-                                    + [(-1.0, e.get((a, r, b, source)))])
-                    if tile is not None:
-                        new[a, r, b, source] = tile
+                tile = total_of([(u[3 * a + c, r], drive.get((c, r, source))) for c in range(3)]
+                                + [(-1.0, e.get((a, r, source)))])
+                if tile is not None:
+                    new[a, r, source] = tile
         return self.merge(new) if merged else new
 
 
@@ -188,20 +176,20 @@
 
 
 def only(field, source):
-    return {i: t for i, t in field.items() if (i[3] == "free") == source}
-
-
-def pole_chain(at_north, load_e, load_h, load_u, metric, gates):
+    return {i: t for i, t in field.items() if (i[2] == "free") == source}
+
+
+def pole_chain(at_north, load, metric, gates):
     p = PoleRows(at_north, metric, gates)
     deep = range(4) if at_north else range(5)
-    e = {(c, r, b, "free"): load_e(c, r, b) for c in range(3) for r in deep for b in range(2)}
-    h = {(c, r, b, "free"): load_h(c, r, b) for c in range(3) for r in range(4) for b in range(2)}
-    u = {(i, r, b): load_u(i, r, b) for i in range(9) for r in range(3 if at_north else 4) for b in range(2)}
+    e = {(c, r, "free"): load("e", c, r) for c in range(3) for r in deep}
+    h = {(c, r, "free"): load("h", c, r) for c in range(3) for r in range(4)}
+    u = {(i, r): v for r in range(3 if at_north else 4) for i, v in enumerate(inverse([load("c", i, r) for i in range(9)]))}
     out = {}
 
     def note(n, field, initial=False):
-        for (c, r, b, source), tile in field.items():
-            if r == 0 and b == 0 and c != 1:
+        for (c, r, source), tile in field.items():
+            if r == 0 and c != 1:
                 out[("free", n) if source == "free" else ("response", n) + source, c] = tile
 
     unit = jnp.ones((8, 128), jnp.float32)
@@ -209,9 +197,8 @@
     if at_north:
         note(0, e)
         h = p.forward(e, h, every(range(4)))
-        for b in range(2):
-            h[0, 0, b, (2, 0)] = -NORTH * unit
-            h[2, 0, b, (0, 0)] = NORTH * unit
+        h[0, 0, (2, 0)] = -NORTH * unit
+        h[2, 0, (0, 0)] = NORTH * unit
         def back(e, h, free_rows, rows, wanted=None, merged=True):
             new = {}
             for free, rr in ((True, free_rows), (False, rows)):
@@ -220,12 +207,12 @@
                 new.update({(i, free): t for i, t in d.items()})
             drive = {i: t for (i, _), t in new.items()}
             want = wanted or every(sorted(set(free_rows) | set(rows)))
-            return p.update(u, drive, {i: t for i, t in e.items() if (i[1] in (free_rows if i[3] == "free" else rows))}, want, merged)
+            return p.update(u, drive, {i: t for i, t in e.items() if (i[1] in (free_rows if i[2] == "free" else rows))}, want, merged)
 
         e = back(e, h, range(3), range(1))
         note(1, e)
         h = p.forward(e, h, every(range(3)))
-        h = {i: t for i, t in h.items() if i[3] == "free" or i[1] < 2}
+        h = {i: t for i, t in h.items() if i[2] == "free" or i[1] < 2}
         e = back(e, h, range(2), range(2))
         note(2, e)
         h = p.forward(e, h, every(range(2)))
@@ -235,9 +222,8 @@
         h = p.forward(e, h, every(range(4)))
         note(0, h)
         drive = p.drive(e, h, range(4))
-        for b in range(2):
-            drive[0, 0, b, (2, 0)] = -NORTH * unit
-            drive[2, 0, b, (0, 0)] = NORTH * unit
+        drive[0, 0, (2, 0)] = -NORTH * unit
+        drive[2, 0, (0, 0)] = NORTH * unit
         e = p.update(u, drive, {i: t for i, t in e.items() if i[1] < 4}, every(range(4)))
         h = p.forward(e, {i: t for i, t in h.items() if i[1] < 3}, every(range(3)))
         note(1, h)
@@ -250,6 +236,11 @@
         h = p.forward(e, {i: t for i, t in h.items() if i[1] < 1}, ends, False)
         note(3, h)
     return out
+
+
+def pole_items(at_north):
+    return ([("e", c, r) for c in range(3) for r in range(4 if at_north else 5)] + [("h", c, r) for c in range(3) for r in range(4)]
+            + [("c", i, r) for i in range(9) for r in range(3 if at_north else 4)])
 
 
 def columns(tiles):
@@ -295,7 +286,7 @@
     return caps
 
 
-def kernel(zf, zb, e_in, h_in, c_in, eo_ref, ho_ref, e_ref, h_ref, c_ref, rows_e, rows_h, rows_c, pack, got, got2, ee, hh, uu, mine,
+def kernel(zf_in, zb_in, e_in, h_in, c_in, eo_ref, ho_ref, zf, zb, e_ref, h_ref, c_ref, rows_e, rows_h, rows_c, pack, got, got2, pole_own, pole_pack, pole_got, pole_sum, ee, hh, uu, mine,
            caps, sums, load_sem, send, recv, cap_send, cap_recv, *, bands, lons):
     band, lon = lax.axis_index("band"), lax.axis_index("lon")
     at_south, at_north = band == 0, band == bands - 1
@@ -304,7 +295,7 @@
     east, west = lax.rem(lon + 1, lons), lax.rem(lon + lons - 1, lons)
     pole = jnp.logical_or(at_south, at_north)
 
-    loads = [pltpu.make_async_copy(s, d, load_sem.at[i]) for i, (s, d) in enumerate(((e_in, e_ref), (h_in, h_ref), (c_in, c_ref)))]
+    loads = [pltpu.make_async_copy(s, d, load_sem.at[i]) for i, (s, d) in enumerate(((e_in, e_ref), (h_in, h_ref), (c_in, c_ref), (zf_in, zf), (zb_in, zb)))]
     for load in loads:
         load.start()
 
@@ -387,6 +378,26 @@
 
     loads[0].wait()
     loads[1].wait()
+    poles = ((True, at_north), (False, at_south))
+    refs = {"e": e_ref, "h": h_ref, "c": c_ref}
+
+    def pole_copy(is_north):
+        part = pl.ds(0, (len(pole_items(is_north)) + 1) // 2)
+        return remote(pole_pack.at[part], pole_got.at[part], 18, band, east)
+
+    @pl.when(pole)
+    def _():
+        loads[2].wait()
+
+    for is_north, condition in poles:
+        @pl.when(condition)
+        def _():
+            tiles = [refs[kind][i, pl.ds(0, 8), 7 - r if is_north else r, :] for kind, i, r in pole_items(is_north)]
+            for n, tile in enumerate(tiles):
+                pole_own[n] = tile
+            for n in range(0, len(tiles), 2):
+                pole_pack[n // 2] = jnp.where(lanes < 64, pltpu.roll(tiles[n], 64, 1), tiles[min(n + 1, len(tiles) - 1)])
+
     pack_field(e_ref, 0, 3)
     pack_field(h_ref, 3, 3)
 
@@ -398,11 +409,22 @@
     def _():
         pl.semaphore_wait(barrier, 8)
 
+    for is_north, condition in poles:
+        @pl.when(condition)
+        def _():
+            pole_copy(is_north).start()
+
     send_part(0)
-    loads[2].wait()
+
+    @pl.when(jnp.logical_not(pole))
+    def _():
+        loads[2].wait()
+
     pack_field(c_ref, 6, 9)
     send_part(1)
 
+    loads[3].wait()
+    loads[4].wait()
     metric, factors, gates = [], [], []
     for block in range(2):
         shift = 0 if block == 0 else jnp.where(rows < 4, 8, -8)
@@ -430,7 +452,6 @@
         take_in(0, k, lambda f: e_ref[f, k] if f < 3 else (h_ref[f - 3, k] if f < 6 else c_ref[f - 6, k]))
         return 0
 
-    lax.fori_loop(0, 8, own, 0)
 
     def unpack(block, ref):
         def one(a, _):
@@ -440,11 +461,6 @@
             return 0
         lax.fori_loop(0, 2, one, 0)
 
-    for n in range(2):
-        for copy in to_lon[n]:
-            copy.wait_recv()
-    unpack(1, got)
-
     offsets = sorted(((i // 32, i // 8 % 4, i % 8) for i in range(1, 64)),
                      key=lambda o: -(4 * o[0] + min(o[1], 4 - o[1]) + min(o[2], 8 - o[2])))
 
@@ -455,22 +471,41 @@
                                             device_id=(band, target), device_id_type=MESH)
 
     names = {}
-    for name, is_north, condition in (("north", True, at_north), ("south", False, at_south)):
+    for is_north, condition in poles:
         @pl.when(condition)
         def _():
-            def sub(r):
-                return 7 - r if is_north else r
-            m = [jnp.broadcast_to(metric[0][sub(r) : sub(r) + 1, :], (8, 128)) for r in range(5)]
-            f = [jnp.broadcast_to(factors[0][sub(r) : sub(r) + 1, :], (8, 128)) for r in range(5)]
-            found = pole_chain(is_north, lambda c, r, b: ee[b, c, pl.ds(0, 8), sub(r), :], lambda c, r, b: hh[b, c, pl.ds(1, 8), sub(r), :],
-                               lambda i, r, b: uu[b, i, pl.ds(0, 8), sub(r), :], m, [[x > s for s in (1, 2, 4)] for x in f])
-            names[name] = list(found)
-            mine[...] = columns(list(found.values()))
+            items = pole_items(is_north)
+            place = {item: n for n, item in enumerate(items)}
+            edge = [7 - r if is_north else r for r in range(5)]
+            m = [jnp.broadcast_to(metric[0][r : r + 1, :], (8, 128)) for r in edge]
+            f = [jnp.broadcast_to(factors[0][r : r + 1, :], (8, 128)) for r in edge]
+            g = [[x > k for k in (1, 2, 4)] for x in f]
+
+            def seam(kind, i, r):
+                n = place[kind, i, r]
+                tile = pole_got[n // 2]
+                return jnp.where(lanes < 64, tile if n % 2 == 0 else pltpu.roll(tile, 64, 1), pltpu.roll(pole_own[n], 64, 1))
+
+            inner = pole_chain(is_north, lambda kind, i, r: pole_own[place[kind, i, r]], m, g)
+            names[is_north] = list(inner)
+            for n, tile in enumerate(inner.values()):
+                pole_sum[n] = tile
+            pole_copy(is_north).wait_recv()
+            outer = pole_chain(is_north, seam, m, g)
+            inside = jnp.logical_and(lanes >= 32, lanes < 96)
+            mine[...] = columns([jnp.where(inside, pole_sum[n] + outer[name], 0.0) for n, name in enumerate(names[is_north])])
 
     @pl.when(pole)
     def _():
         for n, offset in enumerate(offsets):
             cap_copy(n, offset).start()
+
+    lax.fori_loop(0, 8, own, 0)
+
+    for n in range(2):
+        for copy in to_lon[n]:
+            copy.wait_recv()
+    unpack(1, got)
 
     @pl.when(inner_north)
     def _():
@@ -499,11 +534,11 @@
     def _():
         pltpu.make_async_copy(caps, caps, cap_recv.at[0]).wait()
 
-    for name, condition in (("north", at_north), ("south", at_south)):
+    for is_north, condition in poles:
         @pl.when(condition)
         def _():
             total = (mine[...] + jnp.sum(caps[...], axis=0)) * (1.0 / (128 * lons))
-            for n, value in enumerate(solve_caps(names[name], total)):
+            for n, value in enumerate(solve_caps(names[is_north], total)):
                 sums[n, 0] = value[0]
                 sums[n, 1] = value[2]
 
@@ -608,30 +643,54 @@
     def _():
         pltpu.make_async_copy(caps, caps, cap_send.at[0]).wait()
 
+    for is_north, condition in poles:
+        @pl.when(condition)
+        def _():
+            pole_copy(is_north).wait_send()
+
+
+def write_out(e_kept, h_kept, e_out, h_out, sem):
+    copies = [pltpu.make_async_copy(e_kept, e_out, sem.at[0]), pltpu.make_async_copy(h_kept, h_out, sem.at[1])]
+    for copy in copies:
+        copy.start()
+    for copy in copies:
+        copy.wait()
+
 
 def solution(mesh):
     bands, lons = mesh.shape["band"], mesh.shape["lon"]
 
     def on_device(e, h, c, zone_factor, zone_bounds):
-        vmem, smem, hbm = (pl.BlockSpec(memory_space=m) for m in (pltpu.VMEM, pltpu.SMEM, pl.ANY))
+        vmem, hbm = (pl.BlockSpec(memory_space=m) for m in (pltpu.VMEM, pltpu.HBM))
         f32 = lambda *shape: pltpu.VMEM(shape, jnp.float32)
-        like = jax.ShapeDtypeStruct(e.shape, e.dtype)
-        return pl.pallas_call(
+        kept = pltpu.VMEM(e.shape, e.dtype)
+        inputs = [pltpu.with_memory_space_constraint(x, pltpu.HBM) for x in (zone_factor, zone_bounds, e, h, c)]
+        fields = pl.pallas_call(
             functools.partial(kernel, bands=bands, lons=lons),
-            out_shape=(like, like),
-            in_specs=[smem, smem, hbm, hbm, hbm],
+            out_shape=(kept, kept),
+            in_specs=[hbm] * 5,
             out_specs=(vmem, vmem),
             scratch_shapes=[
+                pltpu.SMEM(zone_factor.shape, jnp.int32), pltpu.SMEM(zone_bounds.shape, jnp.int32),
                 f32(3, 8, 8, 128), f32(3, 8, 8, 128), f32(9, 8, 8, 128),
                 f32(3, 8, 8, 128), f32(3, 8, 8, 128), f32(9, 8, 8, 128),
                 f32(2, 2 * FIELDS, 8, 128), f32(2, 2 * FIELDS, 8, 128), f32(2, 2 * FIELDS, 8, 128),
+                f32(64, 8, 128), f32(32, 8, 128), f32(32, 8, 128), f32(64, 8, 128),
                 f32(4, 3, 9, 8, 128), f32(4, 3, 9, 8, 128), f32(4, 9, 8, 8, 128),
                 f32(8, 128), f32(lons - 1, 8, 128), f32(STEPS, 2, 8, 128),
-                pltpu.SemaphoreType.DMA((3,)), pltpu.SemaphoreType.DMA((18,)), pltpu.SemaphoreType.DMA((18,)),
+                pltpu.SemaphoreType.DMA((5,)), pltpu.SemaphoreType.DMA((19,)), pltpu.SemaphoreType.DMA((19,)),
                 pltpu.SemaphoreType.DMA((1,)), pltpu.SemaphoreType.DMA((1,)),
             ],
-            compiler_params=pltpu.CompilerParams(collective_id=0, has_side_effects=True, vmem_limit_bytes=32 * 1024 * 1024),
-        )(zone_factor, zone_bounds, e, h, c)
+            compiler_params=pltpu.CompilerParams(collective_id=0, has_side_effects=True, vmem_limit_bytes=60 * 1024 * 1024),
+        )(*inputs)
+        like = jax.ShapeDtypeStruct(e.shape, e.dtype)
+        return pl.pallas_call(
+            write_out,
+            out_shape=(like, like),
+            in_specs=[vmem, vmem],
+            out_specs=(hbm, hbm),
+            scratch_shapes=[pltpu.SemaphoreType.DMA((2,))],
+        )(*(pltpu.with_memory_space_constraint(x, pltpu.VMEM) for x in fields))
 
     spread = P(None, None, "band", "lon")
     return jax.shard_map(on_device, mesh=mesh, in_specs=(spread, spread, spread, P(), P()), out_specs=(spread, spread),

time: 51.5 us -> 42.7 us (0.83)
  local copies, waits for them, and re-layouts: 5.33 us -> 0 us
  Pallas kernels: 45.3 us -> 41.9 us
    unnamed x12 -> x0, local copies, waits for them, and re-layouts: 5.33 us -> none
    pallas_call x1, Pallas kernels: 45.3 us -> 41.2 us  [on_device(): pl.pallas_call(functools.partial(kernel, bands=bands, lons=lons), out_sha...]
    pallas_call x0 -> x1, Pallas kernels: none -> 0.69 us  [on_device(): pl.pallas_call(write_out, out_shape=(like, like), in_specs=[vmem, vmem],...]
where the time goes in v3:
time: 42.7 us; the launch traced here: 42.5 us
  Pallas kernels  41.9 us (98%)
  between operations  0.64 us (1%)
    pallas_call x1, Pallas kernels, on_device(): pl.pallas_call(functools.partial(kernel, bands=bands, lons=lons), out_sha...  41.2 us

profile of v3, /device:TPU:2, one launch (start us, length us, event | category | flops | bytes accessed | tf_op | source)
XLA Modules:
  0.0 42.5 jit_solution(11816600857666047554)
XLA Ops:
  0.6 41.2 %shard_map.68 = (f32[3,8,8,128]{3,2,1,0:T(8,128)S(1)}, f32[3,8,8,128]{3,2,1,0:T(8,128)S(1)}) custom-call(s32[8]{0:T(128)} %zf_in.1, s32[7]{0:T(128)} %zb_in.1, f32[3,8,8,128]{3,2,1,0:T(8,128)} %e_in.1, f32[3,8,8,128]{3,2,1,0:T(8,128)} %h_in.1, f32[9,8,8,128]{3,2,1,0:T(8,128)} %c_in.1), custom_call_target="tpu_custom_call" | custom-call | tf_op jit(solution)/shard_map/pallas_call | solution.py:668
  41.8 0.7 %shard_map.69 = (f32[3,8,8,128]{3,2,1,0:T(8,128)}, f32[3,8,8,128]{3,2,1,0:T(8,128)}) custom-call(f32[3,8,8,128]{3,2,1,0:T(8,128)S(1)} %get-tuple-element.4.e_kept, f32[3,8,8,128]{3,2,1,0:T(8,128)S(1)} %get-tuple-element.5.h_kept), custom_call_target="tpu_custom_call" | custom-call | tf_op jit(solution)/shard_map/pallas_call | solution.py:687

commit v4 on v3

--- a/solution.py
+++ b/solution.py
@@ -287,7 +287,7 @@
 
 
 def kernel(zf_in, zb_in, e_in, h_in, c_in, eo_ref, ho_ref, zf, zb, e_ref, h_ref, c_ref, rows_e, rows_h, rows_c, pack, got, got2, pole_own, pole_pack, pole_got, pole_sum, ee, hh, uu, mine,
-           caps, sums, load_sem, send, recv, cap_send, cap_recv, *, bands, lons):
+           caps, sums, load_sem, send, recv, cap_send, cap_recv, go, *, bands, lons):
     band, lon = lax.axis_index("band"), lax.axis_index("lon")
     at_south, at_north = band == 0, band == bands - 1
     inner_north, inner_south = jnp.logical_not(at_north), jnp.logical_not(at_south)
@@ -401,13 +401,21 @@
     pack_field(e_ref, 0, 3)
     pack_field(h_ref, 3, 3)
 
+    @pl.when(jnp.logical_not(pole))
+    def _():
+        pl.semaphore_wait(barrier, 8)
+
+    @pl.when(band == 1)
+    def _():
+        pl.semaphore_signal(go, inc=1, device_id=(south, lon), device_id_type=MESH)
+
+    @pl.when(band == bands - 2)
+    def _():
+        pl.semaphore_signal(go, inc=1, device_id=(north, lon), device_id_type=MESH)
+
     @pl.when(pole)
     def _():
-        pl.semaphore_wait(barrier, lons - 1 + 3)
-
-    @pl.when(jnp.logical_not(pole))
-    def _():
-        pl.semaphore_wait(barrier, 8)
+        pl.semaphore_wait(go, 1)
 
     for is_north, condition in poles:
         @pl.when(condition)
@@ -462,7 +470,7 @@
         lax.fori_loop(0, 2, one, 0)
 
     offsets = sorted(((i // 32, i // 8 % 4, i % 8) for i in range(1, 64)),
-                     key=lambda o: -(4 * o[0] + min(o[1], 4 - o[1]) + min(o[2], 8 - o[2])))
+                     key=lambda o: 4 * o[0] + min(o[1], 4 - o[1]) + min(o[2], 8 - o[2]))
 
     def cap_copy(n, offset):
         hi, x, z = lon // 32, lax.rem(lon // 8, 4), lax.rem(lon, 8)
@@ -497,6 +505,7 @@
 
     @pl.when(pole)
     def _():
+        pl.semaphore_wait(barrier, lons - 1 + 3)
         for n, offset in enumerate(offsets):
             cap_copy(n, offset).start()
 
@@ -679,7 +688,7 @@
                 f32(4, 3, 9, 8, 128), f32(4, 3, 9, 8, 128), f32(4, 9, 8, 8, 128),
                 f32(8, 128), f32(lons - 1, 8, 128), f32(STEPS, 2, 8, 128),
                 pltpu.SemaphoreType.DMA((5,)), pltpu.SemaphoreType.DMA((19,)), pltpu.SemaphoreType.DMA((19,)),
-                pltpu.SemaphoreType.DMA((1,)), pltpu.SemaphoreType.DMA((1,)),
+                pltpu.SemaphoreType.DMA((1,)), pltpu.SemaphoreType.DMA((1,)), pltpu.SemaphoreType.REGULAR,
             ],
             compiler_params=pltpu.CompilerParams(collective_id=0, has_side_effects=True, vmem_limit_bytes=60 * 1024 * 1024),
         )(*inputs)

time: 42.7 us -> 38.9 us (0.911)
  the two profiles are of different devices: /device:TPU:2 before, /device:TPU:1 now
where the time goes in v4:
time: 38.9 us; the launch traced here: 38.7 us
  Pallas kernels  38.1 us (98%)
  between operations  0.64 us (2%)
    pallas_call x1, Pallas kernels, on_device(): pl.pallas_call(functools.partial(kernel, bands=bands, lons=lons), out_sha...  37.4 us

profile of v4, /device:TPU:1, one launch (start us, length us, event | category | flops | bytes accessed | tf_op | source)
XLA Modules:
  0.0 38.7 jit_solution(2791288242310974982)
XLA Ops:
  0.6 37.4 %shard_map.68 = (f32[3,8,8,128]{3,2,1,0:T(8,128)S(1)}, f32[3,8,8,128]{3,2,1,0:T(8,128)S(1)}) custom-call(s32[8]{0:T(128)} %zf_in.1, s32[7]{0:T(128)} %zb_in.1, f32[3,8,8,128]{3,2,1,0:T(8,128)} %e_in.1, f32[3,8,8,128]{3,2,1,0:T(8,128)} %h_in.1, f32[9,8,8,128]{3,2,1,0:T(8,128)} %c_in.1), custom_call_target="tpu_custom_call" | custom-call | tf_op jit(solution)/shard_map/pallas_call | solution.py:677
  38.0 0.7 %shard_map.69 = (f32[3,8,8,128]{3,2,1,0:T(8,128)}, f32[3,8,8,128]{3,2,1,0:T(8,128)}) custom-call(f32[3,8,8,128]{3,2,1,0:T(8,128)S(1)} %get-tuple-element.4.e_kept, f32[3,8,8,128]{3,2,1,0:T(8,128)S(1)} %get-tuple-element.5.h_kept), custom_call_target="tpu_custom_call" | custom-call | tf_op jit(solution)/shard_map/pallas_call | solution.py:696

commit v5 on v4

--- a/solution.py
+++ b/solution.py
@@ -352,10 +352,15 @@
     fields, conduct = pl.ds(0, 12), pl.ds(12, 18)
     to_lon = [[remote(pack.at[k, part], got.at[k, part], 2 * n + k, band, (west, east)[k]) for k in range(2)]
               for n, part in enumerate((fields, conduct))]
-    to_north = [[remote(pack.at[k, part, pl.ds(8 - d[k], d[k])], got2.at[k, part, pl.ds(8 - d[k], d[k])], 4 + 2 * n + k, north, (west, east)[k])
-                 for k in range(2)] for n, (part, d) in enumerate(((fields, (4, 3)), (conduct, (3, 2))))]
-    to_south = [[remote(pack.at[k, part, pl.ds(0, d[k])], got2.at[k, part, pl.ds(0, d[k])], 8 + 2 * n + k, south, (west, east)[k])
-                 for k in range(2)] for n, (part, d) in enumerate(((fields, (3, 4)), (conduct, (2, 3))))]
+    north_parts = [[(k, part, pl.ds(8 - d[k], d[k]), 4 + 2 * n + k) for k in range(2)]
+                   for n, (part, d) in enumerate(((fields, (4, 3)), (conduct, (3, 2))))]
+    south_parts = [[(k, part, pl.ds(0, d[k]), 8 + 2 * n + k) for k in range(2)]
+                   for n, (part, d) in enumerate(((fields, (3, 4)), (conduct, (2, 3))))]
+    odd = lax.rem(band, 2) == 1
+    to_north = [[remote(pack.at[k, p, r], got2.at[k, p, r], i, north, (west, east)[k]) for k, p, r, i in parts] for parts in north_parts]
+    to_south = [[remote(pack.at[k, p, r], got2.at[k, p, r], i, south, (west, east)[k]) for k, p, r, i in parts] for parts in south_parts]
+    on_north = [[remote(got.at[k, p, r], got2.at[k, p, r], i, north, lon) for k, p, r, i in parts] for parts in north_parts]
+    on_south = [[remote(got.at[k, p, r], got2.at[k, p, r], i, south, lon) for k, p, r, i in parts] for parts in south_parts]
     trio = ((e_ref, rows_e), (h_ref, rows_h), (c_ref, rows_c))
     rows_north = [remote(s.at[:, :, pl.ds(8 - d, d)], t.at[:, :, pl.ds(8 - d, d)], 12 + i, north, lon)
                   for i, ((s, t), d) in enumerate(zip(trio, (4, 4, 3)))]
@@ -368,12 +373,22 @@
 
         @pl.when(inner_north)
         def _():
-            for copy in to_north[n] + (rows_north[:2] if n == 0 else rows_north[2:]):
+            for copy in rows_north[:2] if n == 0 else rows_north[2:]:
                 copy.start()
 
+        @pl.when(jnp.logical_and(inner_north, jnp.logical_or(odd, at_south)))
+        def _():
+            for copy in to_north[n]:
+                copy.start()
+
         @pl.when(inner_south)
         def _():
-            for copy in to_south[n] + (rows_south[:2] if n == 0 else rows_south[2:]):
+            for copy in rows_south[:2] if n == 0 else rows_south[2:]:
+                copy.start()
+
+        @pl.when(jnp.logical_and(inner_south, jnp.logical_or(jnp.logical_not(odd), at_north)))
+        def _():
+            for copy in to_south[n]:
                 copy.start()
 
     loads[0].wait()
@@ -514,6 +529,17 @@
     for n in range(2):
         for copy in to_lon[n]:
             copy.wait_recv()
+
+        @pl.when(jnp.logical_and(odd, inner_north))
+        def _():
+            for copy in on_south[n]:
+                copy.start()
+
+        @pl.when(jnp.logical_and(jnp.logical_not(odd), inner_south))
+        def _():
+            for copy in on_north[n]:
+                copy.start()
+
     unpack(1, got)
 
     @pl.when(inner_north)
@@ -557,15 +583,16 @@
     gates3 = [[jnp.broadcast_to(g, (8, 8, 128)).reshape(64, 128) for g in gs] for gs in gates]
     lane2 = lax.broadcasted_iota(jnp.int32, (64, 128), 1)
 
-    def turn(f, by, axis):
+    def turn(f, by, axis, blocks):
         size = 128 if axis == 2 else 8
         seam = (lane3 if axis == 2 else row3) == (0 if by == 1 else size - 1)
-        moved = [pltpu.roll(x.reshape(64, 128), by % 128, 1).reshape(8, 8, 128) if axis == 2 else pltpu.roll(x, by % 8, 1) for x in f]
         other = (1, 0, 3, 2) if axis == 2 else (2, 3, 0, 1)
-        return [jnp.where(seam, moved[other[b]], moved[b]) for b in range(4)]
+        moved = {b: pltpu.roll(f[b].reshape(64, 128), by % 128, 1).reshape(8, 8, 128) if axis == 2 else pltpu.roll(f[b], by % 8, 1)
+                 for b in range(4) if b in blocks or other[b] in blocks}
+        return {b: jnp.where(seam, moved[other[b]], moved[b]) for b in blocks}
 
     def merge_all(f, store):
-        x = {(b, c): f[b][c].reshape(64, 128) for b in range(4) for c in range(3)}
+        x = {(b, c): f[b][c].reshape(64, 128) for b in f for c in range(3)}
         for level, step in enumerate((1, 2, 4)):
             other = {i: jnp.take_along_axis(v, lane2 ^ step, axis=1) for i, v in x.items()}
             x = {(b, c): v + jnp.where(gates3[b // 2][level], other[b, c], v) for (b, c), v in x.items()}
@@ -575,49 +602,51 @@
     def ghost(n, c):
         return jnp.concatenate([jnp.broadcast_to(sums[n, c // 2, k : k + 1, :].reshape(1, 1, 128), (1, 8, 128)) for k in range(8)])
 
-    def forward(n):
+    def forward(n, blocks):
         f = [[ee[b, c, 0:8] for b in range(4)] for c in range(3)]
         up = [[ee[b, c, 1:9] for b in range(4)] for c in range(2)]
-        fe = {c: turn(f[c], -1, 2) for c in (1, 2)}
-        fn = {c: turn(f[c], -1, 1) for c in (0, 2)}
+        fe = {c: turn(f[c], -1, 2, blocks) for c in (1, 2)}
+        fn = {c: turn(f[c], -1, 1, blocks) for c in (0, 2)}
         cap = jnp.logical_and(row3 == 7, at_north)
         for c in (0, 2):
             value = ghost(n, c)
-            for b in range(2):
-                fn[c][b] = jnp.where(cap, value, fn[c][b])
-        new = []
-        for b in range(4):
+            for b in (0, 1):
+                if b in blocks:
+                    fn[c][b] = jnp.where(cap, value, fn[c][b])
+        new = {}
+        for b in blocks:
             m = metric3[b // 2]
             curl = (NORTH * (fn[2][b] - f[2][b]) - RADIAL * (up[1][b] - f[1][b]),
                     RADIAL * (up[0][b] - f[0][b]) - m * (fe[2][b] - f[2][b]),
                     m * (fe[1][b] - f[1][b]) - NORTH * (fn[0][b] - f[0][b]))
-            new.append([hh[b, c, 1:9] - curl[c] for c in range(3)])
+            new[b] = [hh[b, c, 1:9] - curl[c] for c in range(3)]
 
         def store(b, c, v):
             hh[b, c, 1:9] = v
 
         merge_all(new, store)
 
-    def backward(n):
+    def backward(n, blocks):
         f = [[hh[b, c, 1:9] for b in range(4)] for c in range(3)]
         down = [[hh[b, c, 0:8] for b in range(4)] for c in range(2)]
-        fw = {c: turn(f[c], 1, 2) for c in (1, 2)}
-        fs = {c: turn(f[c], 1, 1) for c in (0, 2)}
+        fw = {c: turn(f[c], 1, 2, blocks) for c in (1, 2)}
+        fs = {c: turn(f[c], 1, 1, blocks) for c in (0, 2)}
         cap = jnp.logical_and(row3 == 0, at_south)
         for c in (0, 2):
             value = ghost(n, c)
-            for b in range(2):
-                fs[c][b] = jnp.where(cap, value, fs[c][b])
-        new = []
-        for b in range(4):
+            for b in (0, 1):
+                if b in blocks:
+                    fs[c][b] = jnp.where(cap, value, fs[c][b])
+        new = {}
+        for b in blocks:
             m = metric3[b // 2]
             curl = (NORTH * (f[2][b] - fs[2][b]) - RADIAL * (f[1][b] - down[1][b]),
                     RADIAL * (f[0][b] - down[0][b]) - m * (f[2][b] - fw[2][b]),
                     m * (f[1][b] - fw[1][b]) - NORTH * (f[0][b] - fs[0][b]))
             old = [ee[b, c, 0:8] for c in range(3)]
             drive = [2.0 * old[c] + curl[c] for c in range(3)]
-            new.append([uu[b, 3 * a, 0:8] * drive[0] + uu[b, 3 * a + 1, 0:8] * drive[1] + uu[b, 3 * a + 2, 0:8] * drive[2] - old[a]
-                        for a in range(3)])
+            new[b] = [uu[b, 3 * a, 0:8] * drive[0] + uu[b, 3 * a + 1, 0:8] * drive[1] + uu[b, 3 * a + 2, 0:8] * drive[2] - old[a]
+                      for a in range(3)]
 
         def store(b, c, v):
             ee[b, c, 0:8] = v
@@ -625,11 +654,13 @@
         merge_all(new, store)
 
     def step(n, _):
-        forward(n)
-        backward(n)
+        forward(n, range(4))
+        backward(n, range(4))
         return 0
 
-    lax.fori_loop(0, STEPS, step, 0)
+    lax.fori_loop(0, STEPS - 1, step, 0)
+    forward(STEPS - 1, range(3))
+    backward(STEPS - 1, range(1))
     for c in range(3):
         eo_ref[c] = ee[0, c, pl.ds(0, 8)]
         ho_ref[c] = hh[0, c, pl.ds(1, 8)]

time: 38.9 us -> 37.2 us (0.956)
  Pallas kernels: 38.1 us -> 36.4 us
    pallas_call x1, Pallas kernels: 37.4 us -> 35.7 us  [on_device(): pl.pallas_call(functools.partial(kernel, bands=bands, lons=lons), out_sha...]
where the time goes in v5:
time: 37.2 us; the launch traced here: 37 us
  Pallas kernels  36.4 us (98%)
  between operations  0.64 us (2%)
    pallas_call x1, Pallas kernels, on_device(): pl.pallas_call(functools.partial(kernel, bands=bands, lons=lons), out_sha...  35.7 us

profile of v5, /device:TPU:1, one launch (start us, length us, event | category | flops | bytes accessed | tf_op | source)
XLA Modules:
  0.0 37.0 jit_solution(6805121397570565899)
XLA Ops:
  0.6 35.7 %shard_map.68 = (f32[3,8,8,128]{3,2,1,0:T(8,128)S(1)}, f32[3,8,8,128]{3,2,1,0:T(8,128)S(1)}) custom-call(s32[8]{0:T(128)} %zf_in.1, s32[7]{0:T(128)} %zb_in.1, f32[3,8,8,128]{3,2,1,0:T(8,128)} %e_in.1, f32[3,8,8,128]{3,2,1,0:T(8,128)} %h_in.1, f32[9,8,8,128]{3,2,1,0:T(8,128)} %c_in.1), custom_call_target="tpu_custom_call" | custom-call | tf_op jit(solution)/shard_map/pallas_call | solution.py:708
  36.3 0.7 %shard_map.69 = (f32[3,8,8,128]{3,2,1,0:T(8,128)}, f32[3,8,8,128]{3,2,1,0:T(8,128)}) custom-call(f32[3,8,8,128]{3,2,1,0:T(8,128)S(1)} %get-tuple-element.4.e_kept, f32[3,8,8,128]{3,2,1,0:T(8,128)S(1)} %get-tuple-element.5.h_kept), custom_call_target="tpu_custom_call" | custom-call | tf_op jit(solution)/shard_map/pallas_call | solution.py:727

commit v6 on v5

--- a/solution.py
+++ b/solution.py
@@ -10,7 +10,6 @@
 MESH = pl.DeviceIdType.MESH
 STEPS = 4
 NORTH, RADIAL, EAST, FLOOR = 0.45, 0.5, 0.12, 0.25
-FIELDS = 15
 
 
 def lane_ids():
@@ -326,30 +325,36 @@
 
     lanes, rows = lane_ids(), row_ids()
 
-    def pack_field(ref, first, count):
-        def one(i, _):
-            tiles = [(c, a) for c in range(3) for a in range(2)]
-            rolled = [[roll(ref[i * 3 + c, a * 4 + q], 32 * q, 1) for q in range(4)] for c, a in tiles]
-            for n, t in enumerate(rolled):
-                lo, hi = t[0], t[1]
-                for q in range(1, 4):
-                    lo = jnp.where(lanes // 32 == q, t[q], lo)
-                    if q > 1:
-                        hi = jnp.where(lanes // 32 == q - 1, t[q], hi)
-                hi = jnp.where(lanes // 32 == 3, t[0], hi)
-                pack[0, first * 2 + i * 6 + n] = lo
-                pack[1, first * 2 + i * 6 + n] = hi
-            return 0
-        if count == 3:
-            one(0, 0)
-        else:
-            lax.fori_loop(0, count // 3, one, 0)
+    def pack_field(ref, first):
+        rolled = [[roll(ref[c, a * 4 + q], 32 * q, 1) for q in range(4)] for c in range(3) for a in range(2)]
+        for n, t in enumerate(rolled):
+            lo, hi = t[0], t[1]
+            for q in range(1, 4):
+                lo = jnp.where(lanes // 32 == q, t[q], lo)
+                if q > 1:
+                    hi = jnp.where(lanes // 32 == q - 1, t[q], hi)
+            pack[0, first + n] = lo
+            pack[1, first + n] = jnp.where(lanes // 32 == 3, t[0], hi)
+
+    def at_slot(s):
+        return jnp.logical_and(lanes >= 24 * s, lanes < 24 * s + 24)
+
+    def pack_conduct():
+        for tile in range(15):
+            blocks = [divmod(n, 8) for n in range(5 * tile, min(5 * tile + 5, 72))]
+            rolled = [roll(c_ref[i, k], 24 * s, 1) for s, (i, k) in enumerate(blocks)]
+            lo = hi = rolled[0]
+            for s in range(1, len(rolled)):
+                lo = jnp.where(at_slot(s), rolled[s], lo)
+                hi = jnp.where(at_slot(s - 1), rolled[s], hi)
+            pack[0, 12 + tile] = lo
+            pack[1, 12 + tile] = hi
 
     def remote(src, dst, i, b, l):
         return pltpu.make_async_remote_copy(src_ref=src, dst_ref=dst, send_sem=send.at[i], recv_sem=recv.at[i],
                                             device_id=(b, l), device_id_type=MESH)
 
-    fields, conduct = pl.ds(0, 12), pl.ds(12, 18)
+    fields, conduct = pl.ds(0, 12), pl.ds(12, 15)
     to_lon = [[remote(pack.at[k, part], got.at[k, part], 2 * n + k, band, (west, east)[k]) for k in range(2)]
               for n, part in enumerate((fields, conduct))]
     north_parts = [[(k, part, pl.ds(8 - d[k], d[k]), 4 + 2 * n + k) for k in range(2)]
@@ -413,8 +418,8 @@
             for n in range(0, len(tiles), 2):
                 pole_pack[n // 2] = jnp.where(lanes < 64, pltpu.roll(tiles[n], 64, 1), tiles[min(n + 1, len(tiles) - 1)])
 
-    pack_field(e_ref, 0, 3)
-    pack_field(h_ref, 3, 3)
+    pack_field(e_ref, 0)
+    pack_field(h_ref, 6)
 
     @pl.when(jnp.logical_not(pole))
     def _():
@@ -443,7 +448,7 @@
     def _():
         loads[2].wait()
 
-    pack_field(c_ref, 6, 9)
+    pack_conduct()
     send_part(1)
 
     loads[3].wait()
@@ -477,21 +482,22 @@
 
 
     def unpack(block, ref):
-        def one(a, _):
-            for q in range(4):
-                tiles = [roll(jnp.where(lanes // 32 == q, ref[0, 2 * f + a], ref[1, 2 * f + a]), -32 * q, 1) for f in range(FIELDS)]
-                take_in(block, a * 4 + q, lambda f: tiles[f])
-            return 0
-        lax.fori_loop(0, 2, one, 0)
-
-    offsets = sorted(((i // 32, i // 8 % 4, i % 8) for i in range(1, 64)),
-                     key=lambda o: 4 * o[0] + min(o[1], 4 - o[1]) + min(o[2], 8 - o[2]))
-
-    def cap_copy(n, offset):
-        hi, x, z = lon // 32, lax.rem(lon // 8, 4), lax.rem(lon, 8)
-        target = lax.rem(hi + offset[0], 2) * 32 + lax.rem(x + offset[1], 4) * 8 + lax.rem(z + offset[2], 8)
-        return pltpu.make_async_remote_copy(src_ref=mine, dst_ref=caps.at[n], send_sem=cap_send.at[0], recv_sem=cap_recv.at[0],
-                                            device_id=(band, target), device_id_type=MESH)
+        for k in range(8):
+            a, q = divmod(k, 4)
+            tiles = [roll(jnp.where(lanes // 32 == q, ref[0, 2 * f + a], ref[1, 2 * f + a]), -32 * q, 1) for f in range(6)]
+            for i in range(9):
+                tile, slot = divmod(8 * i + k, 5)
+                tiles.append(roll(jnp.where(at_slot(slot), ref[0, 12 + tile], ref[1, 12 + tile]), -24 * slot, 1))
+            take_in(block, k, lambda f: tiles[f])
+
+    near = sorted(((i // 4, i % 4) for i in range(8)), key=lambda o: 4 * o[0] + min(o[1], 4 - o[1]))
+    z_here = lax.rem(lon, 8)
+
+    def cap_copy(z, n):
+        hi, x = lax.rem(lon // 32 + near[n][0], 2), lax.rem(lax.rem(lon // 8, 4) + near[n][1], 4)
+        slot = lax.rem(z - z_here + 8, 8) * 8 + n - 1
+        return pltpu.make_async_remote_copy(src_ref=mine, dst_ref=caps.at[slot], send_sem=cap_send.at[0], recv_sem=cap_recv.at[0],
+                                            device_id=(band, hi * 32 + x * 8 + z), device_id_type=MESH)
 
     names = {}
     for is_north, condition in poles:
@@ -521,8 +527,13 @@
     @pl.when(pole)
     def _():
         pl.semaphore_wait(barrier, lons - 1 + 3)
-        for n, offset in enumerate(offsets):
-            cap_copy(n, offset).start()
+        for z in range(8):
+            @pl.when(z_here != z)
+            def _():
+                cap_copy(z, 0).start()
+
+            for n in range(1, 8):
+                cap_copy(z, n).start()
 
     lax.fori_loop(0, 8, own, 0)
 
@@ -714,7 +725,7 @@
                 pltpu.SMEM(zone_factor.shape, jnp.int32), pltpu.SMEM(zone_bounds.shape, jnp.int32),
                 f32(3, 8, 8, 128), f32(3, 8, 8, 128), f32(9, 8, 8, 128),
                 f32(3, 8, 8, 128), f32(3, 8, 8, 128), f32(9, 8, 8, 128),
-                f32(2, 2 * FIELDS, 8, 128), f32(2, 2 * FIELDS, 8, 128), f32(2, 2 * FIELDS, 8, 128),
+                f32(2, 27, 8, 128), f32(2, 27, 8, 128), f32(2, 27, 8, 128),
                 f32(64, 8, 128), f32(32, 8, 128), f32(32, 8, 128), f32(64, 8, 128),
                 f32(4, 3, 9, 8, 128), f32(4, 3, 9, 8, 128), f32(4, 9, 8, 8, 128),
                 f32(8, 128), f32(lons - 1, 8, 128), f32(STEPS, 2, 8, 128),

time: 37.2 us -> 36.4 us (0.978)
  Pallas kernels: 36.4 us -> 35.6 us
    pallas_call x1, Pallas kernels: 35.7 us -> 34.9 us  [on_device(): pl.pallas_call(functools.partial(kernel, bands=bands, lons=lons), out_sha...]
where the time goes in v6:
time: 36.4 us; the launch traced here: 36.2 us
  Pallas kernels  35.6 us (98%)
  between operations  0.64 us (2%)
    pallas_call x1, Pallas kernels, on_device(): pl.pallas_call(functools.partial(kernel, bands=bands, lons=lons), out_sha...  34.9 us

profile of v6, /device:TPU:1, one launch (start us, length us, event | category | flops | bytes accessed | tf_op | source)
XLA Modules:
  0.0 36.2 jit_solution(8802356955248052391)
XLA Ops:
  0.6 34.9 %shard_map.68 = (f32[3,8,8,128]{3,2,1,0:T(8,128)S(1)}, f32[3,8,8,128]{3,2,1,0:T(8,128)S(1)}) custom-call(s32[8]{0:T(128)} %zf_in.1, s32[7]{0:T(128)} %zb_in.1, f32[3,8,8,128]{3,2,1,0:T(8,128)} %e_in.1, f32[3,8,8,128]{3,2,1,0:T(8,128)} %h_in.1, f32[9,8,8,128]{3,2,1,0:T(8,128)} %c_in.1), custom_call_target="tpu_custom_call" | custom-call | tf_op jit(solution)/shard_map/pallas_call | solution.py:719
  35.5 0.7 %shard_map.69 = (f32[3,8,8,128]{3,2,1,0:T(8,128)}, f32[3,8,8,128]{3,2,1,0:T(8,128)}) custom-call(f32[3,8,8,128]{3,2,1,0:T(8,128)S(1)} %get-tuple-element.4.e_kept, f32[3,8,8,128]{3,2,1,0:T(8,128)S(1)} %get-tuple-element.5.h_kept), custom_call_target="tpu_custom_call" | custom-call | tf_op jit(solution)/shard_map/pallas_call | solution.py:738

commit v7 on v6

--- a/solution.py
+++ b/solution.py
@@ -373,7 +373,7 @@
                   for i, ((s, t), d) in enumerate(zip(trio, (4, 3, 3)))]
 
     def send_part(n):
-        for copy in to_lon[n]:
+        for copy in reversed(to_lon[n]):
             copy.start()
 
         @pl.when(inner_north)
@@ -463,16 +463,18 @@
     zero = jnp.zeros((8, 128), jnp.float32)
     for b in range(4):
         for c in range(3):
-            ee[b, c, 8] = zero
-            hh[b, c, 0] = zero
+            for field in (ee, hh):
+                field[b, c, 0:8] = zero
+                field[b, c, 72:80] = zero
     for n in range(STEPS):
         for i in range(2):
             sums[n, i] = zero
 
     def take_in(block, layer, load):
         for c in range(3):
-            ee[block, c, layer] = load(c)
-            hh[block, c, layer + 1] = load(3 + c)
+            place = pl.ds(8 * layer + 8 if isinstance(layer, int) else pl.multiple_of(8 * layer + 8, 8), 8)
+            ee[block, c, place] = load(c)
+            hh[block, c, place] = load(3 + c)
         for i, value in enumerate(inverse([load(6 + c) for c in range(9)])):
             uu[block, i, layer] = value
 
@@ -594,13 +596,19 @@
     gates3 = [[jnp.broadcast_to(g, (8, 8, 128)).reshape(64, 128) for g in gs] for gs in gates]
     lane2 = lax.broadcasted_iota(jnp.int32, (64, 128), 1)
 
-    def turn(f, by, axis, blocks):
-        size = 128 if axis == 2 else 8
-        seam = (lane3 if axis == 2 else row3) == (0 if by == 1 else size - 1)
-        other = (1, 0, 3, 2) if axis == 2 else (2, 3, 0, 1)
-        moved = {b: pltpu.roll(f[b].reshape(64, 128), by % 128, 1).reshape(8, 8, 128) if axis == 2 else pltpu.roll(f[b], by % 8, 1)
+    def layers(ref, b, c, start=8):
+        return ref[b, c, start : start + 64].reshape(8, 8, 128)
+
+    def turn(f, by, blocks):
+        seam = lane3 == (0 if by == 1 else 127)
+        other = (1, 0, 3, 2)
+        moved = {b: pltpu.roll(f[b].reshape(64, 128), by % 128, 1).reshape(8, 8, 128)
                  for b in range(4) if b in blocks or other[b] in blocks}
         return {b: jnp.where(seam, moved[other[b]], moved[b]) for b in blocks}
+
+    def turn_rows(ref, c, by, blocks):
+        seam = row3 == (0 if by == 1 else 7)
+        return {b: jnp.where(seam, layers(ref, (2, 3, 0, 1)[b], c, 8 + 7 * by), layers(ref, b, c, 8 - by)) for b in blocks}
 
     def merge_all(f, store):
         x = {(b, c): f[b][c].reshape(64, 128) for b in f for c in range(3)}
@@ -608,16 +616,16 @@
             other = {i: jnp.take_along_axis(v, lane2 ^ step, axis=1) for i, v in x.items()}
             x = {(b, c): v + jnp.where(gates3[b // 2][level], other[b, c], v) for (b, c), v in x.items()}
         for (b, c), v in x.items():
-            store(b, c, (v * 0.125).reshape(8, 8, 128))
+            store(b, c, v * 0.125)
 
     def ghost(n, c):
         return jnp.concatenate([jnp.broadcast_to(sums[n, c // 2, k : k + 1, :].reshape(1, 1, 128), (1, 8, 128)) for k in range(8)])
 
     def forward(n, blocks):
-        f = [[ee[b, c, 0:8] for b in range(4)] for c in range(3)]
-        up = [[ee[b, c, 1:9] for b in range(4)] for c in range(2)]
-        fe = {c: turn(f[c], -1, 2, blocks) for c in (1, 2)}
-        fn = {c: turn(f[c], -1, 1, blocks) for c in (0, 2)}
+        f = [[layers(ee, b, c) for b in range(4)] for c in range(3)]
+        up = [[layers(ee, b, c, 16) for b in range(4)] for c in range(2)]
+        fe = {c: turn(f[c], -1, blocks) for c in (1, 2)}
+        fn = {c: turn_rows(ee, c, -1, blocks) for c in (0, 2)}
         cap = jnp.logical_and(row3 == 7, at_north)
         for c in (0, 2):
             value = ghost(n, c)
@@ -630,18 +638,18 @@
             curl = (NORTH * (fn[2][b] - f[2][b]) - RADIAL * (up[1][b] - f[1][b]),
                     RADIAL * (up[0][b] - f[0][b]) - m * (fe[2][b] - f[2][b]),
                     m * (fe[1][b] - f[1][b]) - NORTH * (fn[0][b] - f[0][b]))
-            new[b] = [hh[b, c, 1:9] - curl[c] for c in range(3)]
+            new[b] = [layers(hh, b, c) - curl[c] for c in range(3)]
 
         def store(b, c, v):
-            hh[b, c, 1:9] = v
+            hh[b, c, 8:72] = v
 
         merge_all(new, store)
 
     def backward(n, blocks):
-        f = [[hh[b, c, 1:9] for b in range(4)] for c in range(3)]
-        down = [[hh[b, c, 0:8] for b in range(4)] for c in range(2)]
-        fw = {c: turn(f[c], 1, 2, blocks) for c in (1, 2)}
-        fs = {c: turn(f[c], 1, 1, blocks) for c in (0, 2)}
+        f = [[layers(hh, b, c) for b in range(4)] for c in range(3)]
+        down = [[layers(hh, b, c, 0) for b in range(4)] for c in range(2)]
+        fw = {c: turn(f[c], 1, blocks) for c in (1, 2)}
+        fs = {c: turn_rows(hh, c, 1, blocks) for c in (0, 2)}
         cap = jnp.logical_and(row3 == 0, at_south)
         for c in (0, 2):
             value = ghost(n, c)
@@ -654,13 +662,13 @@
             curl = (NORTH * (f[2][b] - fs[2][b]) - RADIAL * (f[1][b] - down[1][b]),
                     RADIAL * (f[0][b] - down[0][b]) - m * (f[2][b] - fw[2][b]),
                     m * (f[1][b] - fw[1][b]) - NORTH * (f[0][b] - fs[0][b]))
-            old = [ee[b, c, 0:8] for c in range(3)]
+            old = [layers(ee, b, c) for c in range(3)]
             drive = [2.0 * old[c] + curl[c] for c in range(3)]
             new[b] = [uu[b, 3 * a, 0:8] * drive[0] + uu[b, 3 * a + 1, 0:8] * drive[1] + uu[b, 3 * a + 2, 0:8] * drive[2] - old[a]
                       for a in range(3)]
 
         def store(b, c, v):
-            ee[b, c, 0:8] = v
+            ee[b, c, 8:72] = v
 
         merge_all(new, store)
 
@@ -673,8 +681,8 @@
     forward(STEPS - 1, range(3))
     backward(STEPS - 1, range(1))
     for c in range(3):
-        eo_ref[c] = ee[0, c, pl.ds(0, 8)]
-        ho_ref[c] = hh[0, c, pl.ds(1, 8)]
+        eo_ref[c] = layers(ee, 0, c)
+        ho_ref[c] = layers(hh, 0, c)
 
     for n in range(2):
         for copy in to_lon[n]:
@@ -727,7 +735,7 @@
                 f32(3, 8, 8, 128), f32(3, 8, 8, 128), f32(9, 8, 8, 128),
                 f32(2, 27, 8, 128), f32(2, 27, 8, 128), f32(2, 27, 8, 128),
                 f32(64, 8, 128), f32(32, 8, 128), f32(32, 8, 128), f32(64, 8, 128),
-                f32(4, 3, 9, 8, 128), f32(4, 3, 9, 8, 128), f32(4, 9, 8, 8, 128),
+                f32(4, 3, 80, 128), f32(4, 3, 80, 128), f32(4, 9, 8, 8, 128),
                 f32(8, 128), f32(lons - 1, 8, 128), f32(STEPS, 2, 8, 128),
                 pltpu.SemaphoreType.DMA((5,)), pltpu.SemaphoreType.DMA((19,)), pltpu.SemaphoreType.DMA((19,)),
                 pltpu.SemaphoreType.DMA((1,)), pltpu.SemaphoreType.DMA((1,)), pltpu.SemaphoreType.REGULAR,

time: 36.4 us -> 36.4 us (level)
  no operation moved by 1% of the time
where the time goes in v7:
time: 36.4 us; the launch traced here: 36.2 us
  Pallas kernels  35.6 us (98%)
  between operations  0.64 us (2%)
    pallas_call x1, Pallas kernels, on_device(): pl.pallas_call(functools.partial(kernel, bands=bands, lons=lons), out_sha...  34.9 us

profile of v7, /device:TPU:1, one launch (start us, length us, event | category | flops | bytes accessed | tf_op | source)
XLA Modules:
  0.0 36.2 jit_solution(11265074688314218099)
XLA Ops:
  0.6 34.9 %shard_map.68 = (f32[3,8,8,128]{3,2,1,0:T(8,128)S(1)}, f32[3,8,8,128]{3,2,1,0:T(8,128)S(1)}) custom-call(s32[8]{0:T(128)} %zf_in.1, s32[7]{0:T(128)} %zb_in.1, f32[3,8,8,128]{3,2,1,0:T(8,128)} %e_in.1, f32[3,8,8,128]{3,2,1,0:T(8,128)} %h_in.1, f32[9,8,8,128]{3,2,1,0:T(8,128)} %c_in.1), custom_call_target="tpu_custom_call" | custom-call | tf_op jit(solution)/shard_map/pallas_call | solution.py:727
  35.5 0.7 %shard_map.69 = (f32[3,8,8,128]{3,2,1,0:T(8,128)}, f32[3,8,8,128]{3,2,1,0:T(8,128)}) custom-call(f32[3,8,8,128]{3,2,1,0:T(8,128)S(1)} %get-tuple-element.4.e_kept, f32[3,8,8,128]{3,2,1,0:T(8,128)S(1)} %get-tuple-element.5.h_kept), custom_call_target="tpu_custom_call" | custom-call | tf_op jit(solution)/shard_map/pallas_call | solution.py:746
